TPU v7x, 512 devices: a whole 4x4x16 slice. The times are simulated.
512 devices in a mesh: ctx: 256 (over y_hi, z, x, core), head: 2 (over y_lo).
Axes of the slice: x: 4, y: 4 (y_hi: 2, y_lo: 2; y = y_hi * 2 + y_lo), z: 16, core: 2. Of those that a mesh axis runs over, the one named last changes fastest.
Arguments:
- queries: bfloat16 [65536, 4096], P('ctx', 'head')
- keys: bfloat16 [65536, 1024], P(('ctx', 'head'))
- values: bfloat16 [65536, 1024], P(('ctx', 'head')), may hold values from -6 to 6
- segments: int32 [65536], replicated, may hold values from 0 to 127, never falling along the last dimension, each value on 1 to 1024 neighbouring positions
Outputs:
- attended: bfloat16 [65536, 4096], P('ctx', 'head')
Inputs may be any that keep to these rules, and one draw needn't show every extreme that they name: `segments`: ids never fall along the sequence; each document holds 1 to 1024 tokens and one holds exactly 1024.
All inputs are finite; a program needn't handle non-finite values.
Results may differ from a plain program's by a relative error of at most 0.0045.
Values may be sent and summed in bfloat16 or wider, within the bound.
No kernel may reach another device: no remote copies, remote signals or barrier semaphores. Data moves between devices by JAX's collectives and lax.ppermute only.
A program may use at most 64 MiB of HBM per device.

v0:
```python
import jax
import jax.numpy as jnp
from jax import lax
from jax.sharding import PartitionSpec as P

HD = 128


def from_behind(shard, axis, by):
    peers = lax.axis_size(axis)
    pairs = [(i, i + by) for i in range(peers) if 0 <= i + by < peers]
    return lax.ppermute(shard, axis, pairs)


def attend(q_blk, k_blk, v_blk, q_start, k_start, q_seg, k_seg):
    rows = q_blk.shape[0]
    kv_count = k_blk.shape[1] // HD
    group = q_blk.shape[1] // HD // kv_count
    q_pos = q_start + jnp.arange(rows, dtype=jnp.int32)
    k_pos = k_start + jnp.arange(rows, dtype=jnp.int32)
    allowed = (
        (k_pos[None, :] <= q_pos[:, None])
        & (q_pos[:, None] - k_pos[None, :] < 2 * rows)
        & (q_seg[:, None] == k_seg[None, :])
    )
    outs, tops, totals = ([], [], [])
    for head_kv in range(kv_count):
        q_head = q_blk[:, head_kv * group * HD : (head_kv + 1) * group * HD].reshape(
            rows, group, HD
        )
        k_head = k_blk[:, head_kv * HD : (head_kv + 1) * HD]
        v_head = v_blk[:, head_kv * HD : (head_kv + 1) * HD]
        scores = jnp.einsum(
            "qrd,kd->rqk", q_head, k_head, preferred_element_type=jnp.float32
        ) * HD ** (-0.5)
        top = jnp.max(jnp.where(allowed, scores, -1e30), axis=-1)
        prob = jnp.where(allowed, jnp.exp(scores - top[..., None]), 0.0)
        totals.append(jnp.sum(prob, axis=-1))
        tops.append(top)
        outs.append(
            jnp.einsum(
                "rqk,kd->qrd", prob.astype(jnp.bfloat16), v_head, preferred_element_type=jnp.float32
            ).reshape(rows, group * HD)
        )
    return (
        jnp.concatenate(outs, axis=1),
        jnp.concatenate(tops, axis=0),
        jnp.concatenate(totals, axis=0),
    )


def combine(parts):
    highest = parts[0][1]
    for part in parts[1:]:
        highest = jnp.maximum(highest, part[1])
    numer = 0.0
    denom = 0.0
    for outp, top, total in parts:
        weight = jnp.exp(top - highest)
        numer = numer + outp * jnp.repeat(weight.T, HD, axis=1)
        denom = denom + jnp.repeat((weight * total).T, HD, axis=1)
    return (numer / denom).astype(jnp.bfloat16)


def body(queries, keys, values, segments):
    key_local, value_local = (
        lax.all_to_all(keys, "head", split_axis=1, concat_axis=0, tiled=True),
        lax.all_to_all(values, "head", split_axis=1, concat_axis=0, tiled=True),
    )
    rows = queries.shape[0]
    index = lax.axis_index("ctx")
    seg_pad = jnp.concatenate(
        [jnp.full((2 * rows,), -1, jnp.int32), segments, jnp.full((2 * rows,), -2, jnp.int32)]
    )

    def seg_of(block):
        return lax.dynamic_slice_in_dim(seg_pad, (block + 2) * rows, rows)

    own_seg = seg_of(index)
    parts = [attend(queries, key_local, value_local, index * rows, index * rows, own_seg, own_seg)]
    moving_k, moving_v = (key_local, value_local)
    for dist in (1, 2):
        moving_k, moving_v = from_behind((moving_k, moving_v), "ctx", 1)
        parts.append(
            attend(
                queries,
                moving_k,
                moving_v,
                index * rows,
                (index - dist) * rows,
                own_seg,
                seg_of(index - dist),
            )
        )
    return combine(parts)


def solution(mesh):
    placed = (P("ctx", "head"), P(("ctx", "head"), None), P(("ctx", "head"), None), P())
    return jax.shard_map(
        body, mesh=mesh, in_specs=placed, out_specs=P("ctx", "head"), check_vma=False
    )
```

profile of v0, /device:TPU:24, one launch (start us, length us, event | category | flops | bytes accessed | tf_op | source)
XLA Modules:
  0.0 93.7 jit_solution(4711795864547841422)
XLA Ops:
  0.0 1.9 %copy.84 = bf16[128,1024]{0,1:T(8,128)(2,1)} copy(bf16[128,1024]{1,0:T(8,128)(2,1)} %param.6) | data formatting | bytes 524288 | tf_op args[2]
  1.9 4.2 %all-to-all-start.1 = ((bf16[128,2,512]{0,2,1:T(8,128)(2,1)}), bf16[128,2,512]{0,2,1:T(8,128)(2,1)S(1)}, u32[]{:S(2)}, u32[]{:S(2)}) async-start(bf16[128,2,512]{0,2,1:T(8,128)(2,1)} %bitcast.5), calls=%async_computation.1 | async-start | bytes 524288 | tf_op jit(solution)/shard_map/all_to_all | solution.py:68
  6.0 1.7 %copy.168 = bf16[16,2,8,512]{3,2,0,1:T(8,128)(2,1)} copy(bf16[16,2,8,512]{3,2,1,0:T(8,128)(2,1)} %bitcast.239) | data formatting | bytes 524288 | tf_op jit(solution)/shard_map/all_to_all | solution.py:67
  8.4 0.2 copy-done.18
  8.8 0.3 fusion.104
  9.1 0.7 all-to-all-done.1
  9.8 5.2 %all-to-all-start = ((bf16[128,2,512]{2,0,1:T(8,128)(2,1)}), bf16[128,2,512]{2,0,1:T(8,128)(2,1)S(1)}, u32[]{:S(2)}, u32[]{:S(2)}) async-start(bf16[128,2,512]{2,0,1:T(8,128)(2,1)} %bitcast.205), calls=%async_computation | async-start | bytes 524288 | tf_op jit(solution)/shard_map/all_to_all | solution.py:67
  14.9 0.8 copy_bitcast_fusion
  15.7 1.9 %collective-permute-start.2 = (bf16[256,512]{0,1:T(8,128)(2,1)}, bf16[256,512]{0,1:T(8,128)(2,1)}, u32[]{:S(2)}, u32[]{:S(2)}) collective-permute-start(bf16[256,512]{0,1:T(8,128)(2,1)} %copy_bitcast_fusion), channel_id=1, source_target_pairs={{0,2},{2,4},{4,6},{6,8},{8,10},{10,12},{12,14},{14,16},{16,18},{18... | collective-permute-start | bytes 786440 | tf_op jit(solution)/shard_map/ppermute | solution.py:12
  17.6 0.5 all-to-all-done
  18.1 3.0 %collective-permute-start = (bf16[256,512]{1,0:T(8,128)(2,1)S(1)}, bf16[256,512]{1,0:T(8,128)(2,1)}, u32[]{:S(2)}, u32[]{:S(2)}) collective-permute-start(bf16[256,512]{1,0:T(8,128)(2,1)S(1)} %bitcast.234), channel_id=1, source_target_pairs={{0,2},{2,4},{4,6},{6,8},{8,10},{10,12},{12,14},{14,16},{16,18},{18... | collective-permute-start | bytes 786440 | tf_op jit(solution)/shard_map/ppermute | solution.py:12
  21.1 0.3 fusion.12
  21.4 0.3 fusion.11
  21.7 0.3 select_reduce_fusion.11
  22.0 1.2 %fusion.61 = f32[4,256,128]{1,2,0:T(8,128)S(1)} fusion(f32[4,256,256]{1,2,0:T(8,128)S(1)} %get-tuple-element.37, f32[4,256]{1,0:T(4,128)S(1)} %get-tuple-element.36, pred[256,256]{0,1:T(8,128)(4,1)S(1)} %get-tuple-element.35, bf16[256,512]{0,1:T(8,128)(2,1)} %copy_bitcast_fusion), kind=kOutput, calls=%fused_computation.90 | convolution fusion | flops 67895296 | bytes 1708032 | tf_op jit(solution)/shard_map/rqk,kd->qrd/dot_general | solution.py:41
  23.2 1.3 %fusion.15 = (f32[4,256]{1,0:T(4,128)}, f32[4,256]{1,0:T(4,128)S(1)}, f32[4,256]{1,0:T(4,128)S(1)}, f32[4,256]{1,0:T(4,128)S(1)}, f32[4,256,256]{1,2,0:T(8,128)S(1)}) fusion(f32[4,256,256]{1,2,0:T(8,128)S(1)} %get-tuple-element.37, f32[4,256]{1,0:T(4,128)S(1)} %get-tuple-element.36, pred[256,256]{0,1:T(8,128)(4,1)S(1)} %get-tuple-element.35, ...), kind=kOutput, calls=%fused_computation.55 | convolution fusion | flops 69726208 | bytes 4608000 | tf_op jit(solution)/shard_map/qrd,kd->rqk/dot_general | solution.py:33
  24.5 1.2 %fusion.55 = f32[4,256,128]{1,2,0:T(8,128)S(1)} fusion(f32[4,256,256]{1,2,0:T(8,128)S(1)} %fusion.11, f32[4,256]{1,0:T(4,128)S(1)} %get-tuple-element.22, pred[256,256]{0,1:T(8,128)(4,1)S(1)} %get-tuple-element.35, bf16[256,512]{0,1:T(8,128)(2,1)} %copy_bitcast_fusion), kind=kOutput, calls=%fused_computation.87 | convolution fusion | flops 67895296 | bytes 1708032 | tf_op jit(solution)/shard_map/rqk,kd->qrd/dot_general | solution.py:41
  25.7 1.2 %fusion.57 = f32[4,256,128]{1,2,0:T(8,128)S(1)} fusion(f32[4,256,256]{1,2,0:T(8,128)S(1)} %fusion.12, f32[4,256]{1,0:T(4,128)S(1)} %get-tuple-element.21, pred[256,256]{0,1:T(8,128)(4,1)S(1)} %get-tuple-element.35, bf16[256,512]{0,1:T(8,128)(2,1)} %copy_bitcast_fusion), kind=kOutput, calls=%fused_computation.88 | convolution fusion | flops 67895296 | bytes 1708032 | tf_op jit(solution)/shard_map/rqk,kd->qrd/dot_general | solution.py:41
  26.9 1.2 %fusion.17 = (f32[4,256]{1,0:T(4,128)}, f32[4,256]{1,0:T(4,128)}, f32[4,256]{1,0:T(4,128)}) fusion(f32[4,256,256]{1,2,0:T(8,128)S(1)} %get-tuple-element.38, f32[4,256]{1,0:T(4,128)S(1)} %get-tuple-element.20, pred[256,256]{0,1:T(8,128)(4,1)S(1)} %get-tuple-element.35, f32[4,256,256]{1,2,0:T(8,128)S(1)} %fusion.12, f32[4,256]{1,0:T(4,128)S(1)} %get-tuple-element.21, ...), kind=kLoop, calls=%fused_computation.57 | loop fusion | flops 2356224 | bytes 3235840 | tf_op jit(solution)/shard_map/reduce_sum | solution.py:38
  28.0 1.2 %fusion.59 = f32[4,256,128]{1,2,0:T(8,128)S(1)} fusion(f32[4,256,256]{1,2,0:T(8,128)S(1)} %get-tuple-element.38, f32[4,256]{1,0:T(4,128)S(1)} %get-tuple-element.20, pred[256,256]{0,1:T(8,128)(4,1)S(1)} %get-tuple-element.35, bf16[256,512]{0,1:T(8,128)(2,1)} %copy_bitcast_fusion), kind=kOutput, calls=%fused_computation.89 | convolution fusion | flops 67895296 | bytes 1708032 | tf_op jit(solution)/shard_map/rqk,kd->qrd/dot_general | solution.py:41
  29.2 1.0 %copy.96 = f32[256,512]{1,0:T(8,128)} copy(f32[256,512]{0,1:T(8,128)S(1)} %bitcast.222) | data formatting | bytes 1048576 | tf_op jit(solution)/shard_map/reshape | solution.py:43
  30.2 1.0 %copy.97 = f32[256,512]{1,0:T(8,128)} copy(f32[256,512]{0,1:T(8,128)S(1)} %bitcast.225) | data formatting | bytes 1048576 | tf_op jit(solution)/shard_map/reshape | solution.py:43
  31.3 1.0 %copy.98 = f32[256,512]{1,0:T(8,128)} copy(f32[256,512]{0,1:T(8,128)S(1)} %bitcast.224) | data formatting | bytes 1048576 | tf_op jit(solution)/shard_map/reshape | solution.py:43
  32.3 1.0 %copy.99 = f32[256,512]{1,0:T(8,128)} copy(f32[256,512]{0,1:T(8,128)S(1)} %bitcast.223) | data formatting | bytes 1048576 | tf_op jit(solution)/shard_map/reshape | solution.py:43
  33.3 1.8 %collective-permute-done = bf16[256,512]{1,0:T(8,128)(2,1)} collective-permute-done((bf16[256,512]{1,0:T(8,128)(2,1)S(1)}, bf16[256,512]{1,0:T(8,128)(2,1)}, u32[]{:S(2)}, u32[]{:S(2)}) %collective-permute-start) | collective-permute-done | bytes 262176 | tf_op jit(solution)/shard_map/ppermute | solution.py:12
  35.1 1.2 %select_reduce_fusion.7 = (f32[4,256]{1,0:T(4,128)S(1)}, f32[4,256,256]{1,2,0:T(8,128)S(1)}) fusion(pred[256,256]{0,1:T(8,128)(4,1)S(1)} %get-tuple-element.34, bf16[256,4,128]{0,2,1:T(8,128)(2,1)S(1)} %bitcast.214, bf16[256,512]{1,0:T(8,128)(2,1)} %collective-permute-done), kind=kOutput, calls=%fused_computation.46 | convolution fusion | flops 67894272 | bytes 1445888 | tf_op jit(solution)/shard_map/qrd,kd->rqk/dot_general | solution.py:33
  36.3 0.9 %copy-done = f32[4,256,256]{1,2,0:T(8,128)} copy-done((f32[4,256,256]{1,2,0:T(8,128)}, f32[4,256,256]{1,2,0:T(8,128)S(1)}, u32[]{:S(2)}) %copy-start) | copy-done | bytes 1048600
  37.2 1.2 %fusion.53 = f32[4,256,128]{1,2,0:T(8,128)S(1)} fusion(f32[4,256,256]{1,2,0:T(8,128)S(1)} %get-tuple-element.40, f32[4,256]{1,0:T(4,128)S(1)} %get-tuple-element.39, pred[256,256]{0,1:T(8,128)(4,1)S(1)} %get-tuple-element.34, bf16[256,512]{0,1:T(8,128)(2,1)} %collective-permute-done.2), kind=kOutput, calls=%fused_computation.86 | convolution fusion | flops 67895296 | bytes 1708032 | tf_op jit(solution)/shard_map/rqk,kd->qrd/dot_general | solution.py:41
  38.4 1.0 %copy.113 = f32[256,512]{1,0:T(8,128)} copy(f32[256,512]{0,1:T(8,128)S(1)} %bitcast.230) | data formatting | bytes 1048576 | tf_op jit(solution)/shard_map/reshape | solution.py:43
  39.4 1.2 %fusion.8 = f32[4,256,256]{1,2,0:T(8,128)S(1)} fusion(bf16[256,4,128]{0,2,1:T(8,128)(2,1)S(1)} %bitcast.217, bf16[256,512]{1,0:T(8,128)(2,1)} %collective-permute-done), kind=kOutput, calls=%fused_computation.18 | convolution fusion | flops 67371008 | bytes 1376256 | tf_op jit(solution)/shard_map/qrd,kd->rqk/dot_general | solution.py:33
  40.6 1.1 %fusion.7 = f32[4,256,256]{1,2,0:T(8,128)S(1)} fusion(bf16[256,4,128]{0,2,1:T(8,128)(2,1)S(1)} %bitcast.211, bf16[256,512]{1,0:T(8,128)(2,1)} %collective-permute-done), kind=kOutput, calls=%fused_computation.16 | convolution fusion | flops 67371008 | bytes 1376256 | tf_op jit(solution)/shard_map/qrd,kd->rqk/dot_general | solution.py:33
  41.8 2.2 %fusion.23 = (f32[4,256]{1,0:T(4,128)}, f32[4,256]{1,0:T(4,128)S(1)}, f32[4,256]{1,0:T(4,128)}, f32[4,256]{1,0:T(4,128)}, f32[4,256,256]{1,2,0:T(8,128)S(1)}) fusion(f32[4,256,256]{1,2,0:T(8,128)S(1)} %copy-done.1, f32[4,256]{1,0:T(4,128)S(1)} %copy-done.22, pred[256,256]{0,1:T(8,128)(4,1)S(1)} %get-tuple-element.34, f32[4,256,256]{1,2,0:T(8,128)S(1)} %fusion.8, ...), kind=kOutput, calls=%fused_computation.63 | convolution fusion | flops 69726208 | bytes 4608000 | tf_op jit(solution)/shard_map/qrd,kd->rqk/dot_general | solution.py:33
  44.0 0.6 copy-done.24
  44.6 2.0 %fusion.51 = f32[4,256,128]{1,2,0:T(8,128)} fusion(f32[4,256,256]{1,2,0:T(8,128)S(1)} %get-tuple-element.41, f32[4,256]{1,0:T(4,128)S(1)} %get-tuple-element.13, pred[256,256]{0,1:T(8,128)(4,1)S(1)} %get-tuple-element.34, bf16[256,512]{0,1:T(8,128)(2,1)} %collective-permute-done.2), kind=kOutput, calls=%fused_computation.85 | convolution fusion | flops 67895296 | bytes 1708032 | tf_op jit(solution)/shard_map/rqk,kd->qrd/dot_general | solution.py:41
  46.5 2.1 %copy.114 = f32[256,512]{1,0:T(8,128)} copy(f32[256,512]{0,1:T(8,128)} %bitcast.231) | data formatting | bytes 1048576 | tf_op jit(solution)/shard_map/reshape | solution.py:43
  48.6 2.0 %fusion.47 = f32[4,256,128]{1,2,0:T(8,128)} fusion(f32[4,256,256]{1,2,0:T(8,128)S(1)} %fusion.7, f32[4,256]{1,0:T(4,128)} %get-tuple-element.15, pred[256,256]{0,1:T(8,128)(4,1)S(1)} %get-tuple-element.34, bf16[256,512]{0,1:T(8,128)(2,1)} %collective-permute-done.2), kind=kOutput, calls=%fused_computation.83 | convolution fusion | flops 67895296 | bytes 1708032 | tf_op jit(solution)/shard_map/rqk,kd->qrd/dot_general | solution.py:41
  50.6 2.1 %copy.116 = f32[256,512]{1,0:T(8,128)} copy(f32[256,512]{0,1:T(8,128)} %bitcast.232) | data formatting | bytes 1048576 | tf_op jit(solution)/shard_map/reshape | solution.py:43
  52.6 2.0 %fusion.49 = f32[4,256,128]{1,2,0:T(8,128)} fusion(f32[4,256,256]{1,2,0:T(8,128)S(1)} %fusion.8, f32[4,256]{1,0:T(4,128)} %get-tuple-element.14, pred[256,256]{0,1:T(8,128)(4,1)S(1)} %get-tuple-element.34, bf16[256,512]{0,1:T(8,128)(2,1)} %collective-permute-done.2), kind=kOutput, calls=%fused_computation.84 | convolution fusion | flops 67895296 | bytes 1708032 | tf_op jit(solution)/shard_map/rqk,kd->qrd/dot_general | solution.py:41
  54.6 2.0 %copy.115 = f32[256,512]{1,0:T(8,128)} copy(f32[256,512]{0,1:T(8,128)} %bitcast.233) | data formatting | bytes 1048576 | tf_op jit(solution)/shard_map/reshape | solution.py:43
  56.6 2.0 %collective-permute-start.3 = (bf16[256,512]{0,1:T(8,128)(2,1)}, bf16[256,512]{0,1:T(8,128)(2,1)S(1)}, u32[]{:S(2)}, u32[]{:S(2)}) collective-permute-start(bf16[256,512]{0,1:T(8,128)(2,1)} %collective-permute-done.2), channel_id=1, source_target_pairs={{0,2},{2,4},{4,6},{6,8},{8,10},{10,12},{12,14},{14,16},{16,18},{18... | collective-permute-start | bytes 786440 | tf_op jit(solution)/shard_map/ppermute | solution.py:12
  58.7 2.1 %collective-permute-start.1 = (bf16[256,512]{1,0:T(8,128)(2,1)}, bf16[256,512]{1,0:T(8,128)(2,1)S(1)}, u32[]{:S(2)}, u32[]{:S(2)}) collective-permute-start(bf16[256,512]{1,0:T(8,128)(2,1)} %collective-permute-done), channel_id=1, source_target_pairs={{0,2},{2,4},{4,6},{6,8},{8,10},{10,12},{12,14},{14,16},{16,18},{18... | collective-permute-start | bytes 786440 | tf_op jit(solution)/shard_map/ppermute | solution.py:12
  60.8 1.8 %fusion.25 = (f32[4,256]{1,0:T(4,128)}, f32[4,256]{1,0:T(4,128)}, f32[4,256]{1,0:T(4,128)}) fusion(f32[4,256,256]{1,2,0:T(8,128)S(1)} %get-tuple-element.41, f32[4,256]{1,0:T(4,128)} %copy-done.24, pred[256,256]{0,1:T(8,128)(4,1)S(1)} %get-tuple-element.34, f32[4,256,256]{1,2,0:T(8,128)S(1)} %fusion.8, f32[4,256]{1,0:T(4,128)} %get-tuple-element.14, ...), kind=kLoop, calls=%fused_computation.65 | loop fusion | flops 2356224 | bytes 3235840 | tf_op jit(solution)/shard_map/reduce_sum | solution.py:38
  62.6 10.6 %collective-permute-done.1 = bf16[256,512]{1,0:T(8,128)(2,1)S(1)} collective-permute-done((bf16[256,512]{1,0:T(8,128)(2,1)}, bf16[256,512]{1,0:T(8,128)(2,1)S(1)}, u32[]{:S(2)}, u32[]{:S(2)}) %collective-permute-start.1) | collective-permute-done | bytes 262176 | tf_op jit(solution)/shard_map/ppermute | solution.py:12
  73.2 0.3 fusion.4
  73.5 0.3 fusion.3
  73.8 0.3 select_reduce_fusion.3
  74.1 1.3 %fusion.31 = (f32[4,256]{1,0:T(4,128)}, f32[4,256]{1,0:T(4,128)S(1)}, f32[4,256]{1,0:T(4,128)S(1)}, f32[4,256]{1,0:T(4,128)S(1)}, f32[4,256,256]{1,2,0:T(8,128)S(1)}) fusion(f32[4,256,256]{1,2,0:T(8,128)S(1)} %get-tuple-element.43, f32[4,256]{1,0:T(4,128)S(1)} %get-tuple-element.42, pred[256,256]{0,1:T(8,128)(4,1)S(1)} %get-tuple-element.33, ...), kind=kOutput, calls=%fused_computation.71 | convolution fusion | flops 69726208 | bytes 4608000 | tf_op jit(solution)/shard_map/qrd,kd->rqk/dot_general | solution.py:33
  75.5 0.6 fusion.121
  76.2 1.1 %fusion.45 = f32[4,256,128]{1,2,0:T(8,128)} fusion(f32[4,256,256]{1,2,0:T(8,128)S(1)} %get-tuple-element.43, f32[4,256]{1,0:T(4,128)S(1)} %get-tuple-element.42, pred[256,256]{0,1:T(8,128)(4,1)S(1)} %get-tuple-element.33, bf16[256,512]{0,1:T(8,128)(2,1)S(1)} %collective-permute-done.3), kind=kOutput, calls=%fused_computation.82 | convolution fusion | flops 67895296 | bytes 1708032 | tf_op jit(solution)/shard_map/rqk,kd->qrd/dot_general | solution.py:41
  77.3 2.1 %copy.122 = f32[256,512]{1,0:T(8,128)} copy(f32[256,512]{0,1:T(8,128)} %bitcast.227) | data formatting | bytes 1048576 | tf_op jit(solution)/shard_map/reshape | solution.py:43
  79.4 1.2 %fusion.33 = (f32[4,256]{1,0:T(4,128)}, f32[4,256]{1,0:T(4,128)}, f32[4,256]{1,0:T(4,128)}) fusion(f32[4,256,256]{1,2,0:T(8,128)S(1)} %get-tuple-element.44, f32[4,256]{1,0:T(4,128)S(1)} %get-tuple-element.6, pred[256,256]{0,1:T(8,128)(4,1)S(1)} %get-tuple-element.33, f32[4,256,256]{1,2,0:T(8,128)S(1)} %fusion.4, f32[4,256]{1,0:T(4,128)S(1)} %get-tuple-element.7, ...), kind=kLoop, calls=%fused_computation.73 | loop fusion | flops 2356224 | bytes 3235840 | tf_op jit(solution)/shard_map/reduce_sum | solution.py:38
  80.5 1.1 %fusion.43 = f32[4,256,128]{1,2,0:T(8,128)} fusion(f32[4,256,256]{1,2,0:T(8,128)S(1)} %get-tuple-element.44, f32[4,256]{1,0:T(4,128)S(1)} %get-tuple-element.6, pred[256,256]{0,1:T(8,128)(4,1)S(1)} %get-tuple-element.33, bf16[256,512]{0,1:T(8,128)(2,1)S(1)} %copy-done.20), kind=kOutput, calls=%fused_computation.81 | convolution fusion | flops 67895296 | bytes 1708032 | tf_op jit(solution)/shard_map/rqk,kd->qrd/dot_general | solution.py:41
  81.7 1.2 %copy.123 = f32[256,512]{1,0:T(8,128)S(1)} copy(f32[256,512]{0,1:T(8,128)} %bitcast.228) | data formatting | bytes 1048576 | tf_op jit(solution)/shard_map/reshape | solution.py:43
  82.9 1.1 %fusion.39 = f32[4,256,128]{1,2,0:T(8,128)} fusion(f32[4,256,256]{1,2,0:T(8,128)S(1)} %fusion.3, f32[4,256]{1,0:T(4,128)S(1)} %get-tuple-element.8, pred[256,256]{0,1:T(8,128)(4,1)S(1)} %get-tuple-element.33, bf16[256,512]{0,1:T(8,128)(2,1)S(1)} %copy-done.20), kind=kOutput, calls=%fused_computation.79 | convolution fusion | flops 67895296 | bytes 1708032 | tf_op jit(solution)/shard_map/rqk,kd->qrd/dot_general | solution.py:41
  84.1 1.2 %copy.125 = f32[256,512]{1,0:T(8,128)S(1)} copy(f32[256,512]{0,1:T(8,128)} %bitcast.229) | data formatting | bytes 1048576 | tf_op jit(solution)/shard_map/reshape | solution.py:43
  85.4 0.3 fusion.41
  85.7 0.2 copy.124
  86.5 0.6 broadcast_in_dim.120
  87.1 0.6 broadcast_in_dim.119
  87.8 0.6 broadcast_in_dim.117
  88.4 0.6 broadcast_in_dim.118
  89.6 0.2 copy-done.14
  89.8 0.2 copy-done.15
  89.9 3.8 %fusion = bf16[256,2048]{1,0:T(8,128)(2,1)} fusion(f32[32,8,16,128]{3,2,1,0:T(8,128)S(1)} %bitcast.206, f32[32,8,16,128]{3,2,1,0:T(8,128)S(1)} %bitcast.207, f32[32,8,16,128]{3,2,1,0:T(8,128)S(1)} %bitcast.209, f32[32,8,16,128]{3,2,1,0:T(8,128)S(1)} %bitcast.208, f32[256,512]{1,0:T(8,128)S(1)} %copy-done.11, f32[256,512]{1,0:T(8,128)S(1)} %copy-done.10, ...), kind=kLoop, calls=%fused_computation.1 | loop fusion | flops 8388608 | bytes 15728640 | tf_op jit(solution)/shard_map/convert_element_type | solution.py:62
  (96 shorter events, 2.0 us)
Async XLA Ops:
  0.0 7.7 %copy-start.17 = (bf16[256,2048]{1,0:T(8,128)(2,1)S(1)}, bf16[256,2048]{1,0:T(8,128)(2,1)}, u32[]{:S(2)}) copy-start(bf16[256,2048]{1,0:T(8,128)(2,1)} %param.4) | copy-start | bytes 3145732
  1.9 7.9 %all-to-all-start.1 = ((bf16[128,2,512]{0,2,1:T(8,128)(2,1)}), bf16[128,2,512]{0,2,1:T(8,128)(2,1)S(1)}, u32[]{:S(2)}, u32[]{:S(2)}) async-start(bf16[128,2,512]{0,2,1:T(8,128)(2,1)} %bitcast.5), calls=%async_computation.1 | async-start | bytes 524288 | tf_op jit(solution)/shard_map/all_to_all | solution.py:68
  7.7 1.0 %copy-start.18 = (s32[65536]{0:T(1024)S(1)}, s32[65536]{0:T(1024)}, u32[]{:S(2)}) copy-start(s32[65536]{0:T(1024)} %param.7) | copy-start | bytes 786436
  8.1 31.3 %copy-start.4 = (bf16[256,512]{0,1:T(8,128)(2,1)}, bf16[256,512]{0,1:T(8,128)(2,1)S(1)}, u32[]{:S(2)}) copy-start(bf16[256,512]{0,1:T(8,128)(2,1)S(1)} %copy.154) | copy-start | bytes 786436
  8.2 16.3 %copy-start.6 = (bf16[256,512]{0,1:T(8,128)(2,1)}, bf16[256,512]{0,1:T(8,128)(2,1)S(1)}, u32[]{:S(2)}) copy-start(bf16[256,512]{0,1:T(8,128)(2,1)S(1)} %copy.153) | copy-start | bytes 786436
  8.4 26.7 %copy-start.2 = (bf16[256,512]{0,1:T(8,128)(2,1)}, bf16[256,512]{0,1:T(8,128)(2,1)S(1)}, u32[]{:S(2)}) copy-start(bf16[256,512]{0,1:T(8,128)(2,1)S(1)} %copy.152) | copy-start | bytes 786436
  9.8 8.3 %all-to-all-start = ((bf16[128,2,512]{2,0,1:T(8,128)(2,1)}), bf16[128,2,512]{2,0,1:T(8,128)(2,1)S(1)}, u32[]{:S(2)}, u32[]{:S(2)}) async-start(bf16[128,2,512]{2,0,1:T(8,128)(2,1)} %bitcast.205), calls=%async_computation | async-start | bytes 524288 | tf_op jit(solution)/shard_map/all_to_all | solution.py:67
  15.7 20.6 %collective-permute-start.2 = (bf16[256,512]{0,1:T(8,128)(2,1)}, bf16[256,512]{0,1:T(8,128)(2,1)}, u32[]{:S(2)}, u32[]{:S(2)}) collective-permute-start(bf16[256,512]{0,1:T(8,128)(2,1)} %copy_bitcast_fusion), channel_id=1, source_target_pairs={{0,2},{2,4},{4,6},{6,8},{8,10},{10,12},{12,14},{14,16},{16,18},{18... | collective-permute-start | bytes 786440 | tf_op jit(solution)/shard_map/ppermute | solution.py:12
  18.1 17.0 %collective-permute-start = (bf16[256,512]{1,0:T(8,128)(2,1)S(1)}, bf16[256,512]{1,0:T(8,128)(2,1)}, u32[]{:S(2)}, u32[]{:S(2)}) collective-permute-start(bf16[256,512]{1,0:T(8,128)(2,1)S(1)} %bitcast.234), channel_id=1, source_target_pairs={{0,2},{2,4},{4,6},{6,8},{8,10},{10,12},{12,14},{14,16},{16,18},{18... | collective-permute-start | bytes 786440 | tf_op jit(solution)/shard_map/ppermute | solution.py:12
  36.3 1.0 %copy-start = (f32[4,256,256]{1,2,0:T(8,128)}, f32[4,256,256]{1,2,0:T(8,128)S(1)}, u32[]{:S(2)}) copy-start(f32[4,256,256]{1,2,0:T(8,128)S(1)} %get-tuple-element.40) | copy-start | bytes 3145732
  36.3 2.1 %copy-start.21 = (f32[4,256]{1,0:T(4,128)}, f32[4,256]{1,0:T(4,128)S(1)}, u32[]{:S(2)}) copy-start(f32[4,256]{1,0:T(4,128)S(1)} %get-tuple-element.39) | copy-start | bytes 12292
  39.4 2.3 %copy-start.1 = (f32[4,256,256]{1,2,0:T(8,128)S(1)}, f32[4,256,256]{1,2,0:T(8,128)}, u32[]{:S(2)}) copy-start(f32[4,256,256]{1,2,0:T(8,128)} %copy-done) | copy-start | bytes 3145732
  39.4 2.4 %copy-start.22 = (f32[4,256]{1,0:T(4,128)S(1)}, f32[4,256]{1,0:T(4,128)}, u32[]{:S(2)}) copy-start(f32[4,256]{1,0:T(4,128)} %copy-done.21) | copy-start | bytes 12292
  44.0 0.6 copy-start.24
  56.6 16.6 %copy-start.5 = (bf16[256,512]{0,1:T(8,128)(2,1)S(1)}, bf16[256,512]{0,1:T(8,128)(2,1)}, u32[]{:S(2)}) copy-start(bf16[256,512]{0,1:T(8,128)(2,1)} %copy-done.4) | copy-start | bytes 786436
  56.6 19.5 %collective-permute-start.3 = (bf16[256,512]{0,1:T(8,128)(2,1)}, bf16[256,512]{0,1:T(8,128)(2,1)S(1)}, u32[]{:S(2)}, u32[]{:S(2)}) collective-permute-start(bf16[256,512]{0,1:T(8,128)(2,1)} %collective-permute-done.2), channel_id=1, source_target_pairs={{0,2},{2,4},{4,6},{6,8},{8,10},{10,12},{12,14},{14,16},{16,18},{18... | collective-permute-start | bytes 786440 | tf_op jit(solution)/shard_map/ppermute | solution.py:12
  58.7 14.5 %collective-permute-start.1 = (bf16[256,512]{1,0:T(8,128)(2,1)}, bf16[256,512]{1,0:T(8,128)(2,1)S(1)}, u32[]{:S(2)}, u32[]{:S(2)}) collective-permute-start(bf16[256,512]{1,0:T(8,128)(2,1)} %collective-permute-done), channel_id=1, source_target_pairs={{0,2},{2,4},{4,6},{6,8},{8,10},{10,12},{12,14},{14,16},{16,18},{18... | collective-permute-start | bytes 786440 | tf_op jit(solution)/shard_map/ppermute | solution.py:12
  62.6 11.1 %copy-start.3 = (bf16[256,512]{0,1:T(8,128)(2,1)S(1)}, bf16[256,512]{0,1:T(8,128)(2,1)}, u32[]{:S(2)}) copy-start(bf16[256,512]{0,1:T(8,128)(2,1)} %copy-done.2) | copy-start | bytes 786436
  62.6 11.5 %copy-start.7 = (bf16[256,512]{0,1:T(8,128)(2,1)S(1)}, bf16[256,512]{0,1:T(8,128)(2,1)}, u32[]{:S(2)}) copy-start(bf16[256,512]{0,1:T(8,128)(2,1)} %copy-done.6) | copy-start | bytes 786436
  74.1 1.4 %copy-start.23 = (f32[4,256]{1,0:T(4,128)S(1)}, f32[4,256]{1,0:T(4,128)}, u32[]{:S(2)}) copy-start(f32[4,256]{1,0:T(4,128)} %copy-done.21) | copy-start | bytes 12292
  74.1 1.3 %copy-start.25 = (f32[4,256]{1,0:T(4,128)S(1)}, f32[4,256]{1,0:T(4,128)}, u32[]{:S(2)}) copy-start(f32[4,256]{1,0:T(4,128)} %copy-done.24) | copy-start | bytes 12292
  74.1 1.3 %copy-start.26 = (f32[4,256]{1,0:T(4,128)S(1)}, f32[4,256]{1,0:T(4,128)}, u32[]{:S(2)}) copy-start(f32[4,256]{1,0:T(4,128)} %get-tuple-element.14) | copy-start | bytes 12292
  74.1 1.3 %copy-start.27 = (f32[4,256]{1,0:T(4,128)S(1)}, f32[4,256]{1,0:T(4,128)}, u32[]{:S(2)}) copy-start(f32[4,256]{1,0:T(4,128)} %get-tuple-element.15) | copy-start | bytes 12292
  76.1 1.1 %copy-start.19 = (bf16[256,512]{0,1:T(8,128)(2,1)}, bf16[256,512]{0,1:T(8,128)(2,1)S(1)}, u32[]{:S(2)}) copy-start(bf16[256,512]{0,1:T(8,128)(2,1)S(1)} %collective-permute-done.3) | copy-start | bytes 786436
  77.3 3.3 %copy-start.20 = (bf16[256,512]{0,1:T(8,128)(2,1)S(1)}, bf16[256,512]{0,1:T(8,128)(2,1)}, u32[]{:S(2)}) copy-start(bf16[256,512]{0,1:T(8,128)(2,1)} %copy-done.19) | copy-start | bytes 786436
  84.0 1.9 %copy-start.28 = (f32[256,16]{0,1:T(8,128)S(1)}, f32[256,16]{0,1:T(8,128)}, u32[]{:S(2)}) copy-start(f32[256,16]{0,1:T(8,128)} %fusion.121) | copy-start | bytes 49156
  84.0 2.2 %copy-start.29 = (f32[4,256]{1,0:T(4,128)S(1)}, f32[4,256]{1,0:T(4,128)}, u32[]{:S(2)}) copy-start(f32[4,256]{1,0:T(4,128)} %get-tuple-element.23) | copy-start | bytes 12292
  84.0 2.2 %copy-start.30 = (f32[4,256]{1,0:T(4,128)S(1)}, f32[4,256]{1,0:T(4,128)}, u32[]{:S(2)}) copy-start(f32[4,256]{1,0:T(4,128)} %get-tuple-element.24) | copy-start | bytes 12292
  84.0 2.2 %copy-start.31 = (f32[4,256]{1,0:T(4,128)S(1)}, f32[4,256]{1,0:T(4,128)}, u32[]{:S(2)}) copy-start(f32[4,256]{1,0:T(4,128)} %get-tuple-element.25) | copy-start | bytes 12292
  84.1 2.2 %copy-start.32 = (f32[4,256]{1,0:T(4,128)S(1)}, f32[4,256]{1,0:T(4,128)}, u32[]{:S(2)}) copy-start(f32[4,256]{1,0:T(4,128)} %get-tuple-element.16) | copy-start | bytes 12292
  84.1 2.2 %copy-start.33 = (f32[4,256]{1,0:T(4,128)S(1)}, f32[4,256]{1,0:T(4,128)}, u32[]{:S(2)}) copy-start(f32[4,256]{1,0:T(4,128)} %get-tuple-element.17) | copy-start | bytes 12292
  84.1 2.2 %copy-start.34 = (f32[4,256]{1,0:T(4,128)S(1)}, f32[4,256]{1,0:T(4,128)}, u32[]{:S(2)}) copy-start(f32[4,256]{1,0:T(4,128)} %get-tuple-element.18) | copy-start | bytes 12292
  84.1 2.2 %copy-start.35 = (f32[4,256]{1,0:T(4,128)S(1)}, f32[4,256]{1,0:T(4,128)}, u32[]{:S(2)}) copy-start(f32[4,256]{1,0:T(4,128)} %get-tuple-element.9) | copy-start | bytes 12292
  84.1 2.2 %copy-start.36 = (f32[4,256]{1,0:T(4,128)S(1)}, f32[4,256]{1,0:T(4,128)}, u32[]{:S(2)}) copy-start(f32[4,256]{1,0:T(4,128)} %get-tuple-element.10) | copy-start | bytes 12292
  84.1 2.2 %copy-start.37 = (f32[4,256]{1,0:T(4,128)S(1)}, f32[4,256]{1,0:T(4,128)}, u32[]{:S(2)}) copy-start(f32[4,256]{1,0:T(4,128)} %get-tuple-element.11) | copy-start | bytes 12292
  84.1 2.2 %copy-start.38 = (f32[4,256]{1,0:T(4,128)S(1)}, f32[4,256]{1,0:T(4,128)}, u32[]{:S(2)}) copy-start(f32[4,256]{1,0:T(4,128)} %get-tuple-element.19) | copy-start | bytes 12292
  84.1 2.2 %copy-start.39 = (f32[4,256]{1,0:T(4,128)S(1)}, f32[4,256]{1,0:T(4,128)}, u32[]{:S(2)}) copy-start(f32[4,256]{1,0:T(4,128)} %get-tuple-element.12) | copy-start | bytes 12292
  84.1 2.2 %copy-start.40 = (f32[4,256]{1,0:T(4,128)S(1)}, f32[4,256]{1,0:T(4,128)}, u32[]{:S(2)}) copy-start(f32[4,256]{1,0:T(4,128)} %get-tuple-element.5) | copy-start | bytes 12292
  87.1 1.9 %copy-start.16 = (f32[256,512]{1,0:T(8,128)S(1)}, f32[256,512]{1,0:T(8,128)}, u32[]{:S(2)}) copy-start(f32[256,512]{1,0:T(8,128)} %copy.122) | copy-start | bytes 1572868
  87.7 1.3 %copy-start.8 = (f32[256,512]{1,0:T(8,128)S(1)}, f32[256,512]{1,0:T(8,128)}, u32[]{:S(2)}) copy-start(f32[256,512]{1,0:T(8,128)} %copy.96) | copy-start | bytes 1572868
  87.7 1.3 %copy-start.9 = (f32[256,512]{1,0:T(8,128)S(1)}, f32[256,512]{1,0:T(8,128)}, u32[]{:S(2)}) copy-start(f32[256,512]{1,0:T(8,128)} %copy.97) | copy-start | bytes 1572868
  87.7 1.4 %copy-start.10 = (f32[256,512]{1,0:T(8,128)S(1)}, f32[256,512]{1,0:T(8,128)}, u32[]{:S(2)}) copy-start(f32[256,512]{1,0:T(8,128)} %copy.98) | copy-start | bytes 1572868
  87.8 1.5 %copy-start.11 = (f32[256,512]{1,0:T(8,128)S(1)}, f32[256,512]{1,0:T(8,128)}, u32[]{:S(2)}) copy-start(f32[256,512]{1,0:T(8,128)} %copy.99) | copy-start | bytes 1572868
  87.8 1.7 %copy-start.12 = (f32[256,512]{1,0:T(8,128)S(1)}, f32[256,512]{1,0:T(8,128)}, u32[]{:S(2)}) copy-start(f32[256,512]{1,0:T(8,128)} %copy.113) | copy-start | bytes 1572868
  87.8 1.8 %copy-start.13 = (f32[256,512]{1,0:T(8,128)S(1)}, f32[256,512]{1,0:T(8,128)}, u32[]{:S(2)}) copy-start(f32[256,512]{1,0:T(8,128)} %copy.114) | copy-start | bytes 1572868
  87.8 2.0 %copy-start.14 = (f32[256,512]{1,0:T(8,128)S(1)}, f32[256,512]{1,0:T(8,128)}, u32[]{:S(2)}) copy-start(f32[256,512]{1,0:T(8,128)} %copy.116) | copy-start | bytes 1572868
  87.8 2.1 %copy-start.15 = (f32[256,512]{1,0:T(8,128)S(1)}, f32[256,512]{1,0:T(8,128)}, u32[]{:S(2)}) copy-start(f32[256,512]{1,0:T(8,128)} %copy.115) | copy-start | bytes 1572868
where the time goes:
time: 94.8 us; the launch traced here: 93.7 us
  local copies, waits for them, and re-layouts  26.4 us (28%)
  matrix products  25.5 us (27%)
  starting transfers between devices  18.4 us (19%)
  waiting for transfers between devices  13.6 us (14%)
  other arithmetic  9.1 us (10%)
    reshape x12, local copies, waits for them, and re-layouts, attend(): outs.append(jnp.einsum('rqk,kd->qrd', prob.astype(jnp.bfloat16), v_head,...  15.9 us
    dot_general x12, matrix products, attend(): jnp.einsum('rqk,kd->qrd', prob.astype(jnp.bfloat16), v_head, preferred_el...  15.5 us
    ppermute x4, waiting for transfers between devices, from_behind(): return lax.ppermute(shard, axis, pairs)  12.4 us
    dot_general x12, matrix products, attend(): jnp.einsum('qrd,kd->rqk', q_head, k_head, preferred_element_type=jnp.floa...  10 us
    ppermute x4, starting transfers between devices, from_behind(): return lax.ppermute(shard, axis, pairs)  9.07 us
    unnamed x87, local copies, waits for them, and re-layouts  5.18 us
    all_to_all x1, starting transfers between devices, body(): lax.all_to_all(keys, 'head', split_axis=1, concat_axis=0, tiled=True)  5.17 us
    reduce_sum x3, other arithmetic, attend(): totals.append(jnp.sum(prob, axis=-1))  4.18 us
  transfers between devices with their start and end apart: 6, of which 4 were waited for; matrix products, arithmetic and copies ran while one was open for 23% of the time, Pallas kernels for 0%

commit v1 on v0

v1 whole, which is shorter than its diff:
```python
import math
import jax
import jax.numpy as jnp
from jax import lax
from jax.experimental import pallas as pl
from jax.experimental.pallas import tpu as pltpu
from jax.sharding import PartitionSpec as P

HD = 128
HALF = 128
WINDOW = 512
BOTH = ("ctx", "head")
EXP2_SCALE = HD ** (-0.5) * math.log2(math.e)


def attention_kernel(seg_ref, q_ref, a0, b0, a1, b1, a2, b2, out_ref, bias_ref):
    c = lax.axis_index("ctx")
    first = lax.axis_index("head") == 0
    kv_heads = a0.shape[1] // (2 * HD)
    group = q_ref.shape[1] // HD // kv_heads
    halves = 6
    seen = halves - 1

    row = lax.broadcasted_iota(jnp.int32, (HALF, HALF), 0)
    col = lax.broadcasted_iota(jnp.int32, (HALF, HALF), 1)
    for qb in range(2):
        q_seg = jnp.broadcast_to(seg_ref[pl.ds(2 * c + qb, 1), :], (HALF, HALF)).T
        for t in range(seen):
            key_half = 2 * c - 4 + qb + t
            k_seg = seg_ref[pl.ds(jnp.maximum(key_half, 0), 1), :]
            ok = (q_seg == k_seg) & (key_half >= 0)
            if t == seen - 1:
                ok = ok & (col <= row)
            if t == 0:
                ok = ok & (col > row)
            bias_ref[qb, :, t * HALF : (t + 1) * HALF] = jnp.where(ok, 0.0, -jnp.inf)

    ones = jnp.ones((halves * HALF, HD), jnp.bfloat16)
    for g in range(kv_heads):
        def both_halves(near, cross, at):
            x = near[:, at * HD : (at + 1) * HD]
            y = cross[:, at * HD : (at + 1) * HD]
            return [jnp.where(first, x, y), jnp.where(first, y, x)]

        k_all, v_all = [], []
        for near, cross in ((a2, b2), (a1, b1), (a0, b0)):
            k_all += both_halves(near, cross, g)
            v_all += both_halves(near, cross, kv_heads + g)
        k_all = jnp.concatenate(k_all, axis=0)
        v_all = jnp.concatenate([jnp.concatenate(v_all, axis=0), ones], axis=1)
        for qb in range(2):
            rows = slice(qb * HALF, (qb + 1) * HALF)
            q = jnp.concatenate(
                [q_ref[rows, (g * group + r) * HD : (g * group + r + 1) * HD] for r in range(group)], axis=0
            )
            k = k_all[qb * HALF : (qb + seen) * HALF]
            v = v_all[qb * HALF : (qb + seen) * HALF]
            s = lax.dot_general(q, k, (((1,), (1,)), ((), ())), preferred_element_type=jnp.float32)
            s = s.reshape(group, HALF, seen * HALF) + bias_ref[qb][None]
            top = jnp.max(s, axis=-1, keepdims=True)
            p = jnp.exp2((s - top) * EXP2_SCALE).astype(jnp.bfloat16)
            o = jnp.dot(p.reshape(group * HALF, seen * HALF), v, preferred_element_type=jnp.float32)
            o = (o[:, :HD] / o[:, HD:]).astype(jnp.bfloat16)
            for r in range(group):
                out_ref[rows, (g * group + r) * HD : (g * group + r + 1) * HD] = o[r * HALF : (r + 1) * HALF]


def attention(seg, q, *pieces):
    vmem = pl.BlockSpec(memory_space=pltpu.VMEM)
    return pl.pallas_call(
        attention_kernel,
        out_shape=jax.ShapeDtypeStruct(q.shape, q.dtype),
        in_specs=[vmem] * (2 + len(pieces)),
        out_specs=vmem,
        scratch_shapes=[pltpu.VMEM((2, HALF, 5 * HALF), jnp.float32)],
        compiler_params=pltpu.CompilerParams(vmem_limit_bytes=40 * 1024 * 1024),
    )(seg, q, *pieces)


def send(x, by, cross):
    blocks = lax.axis_size("ctx")
    pairs = [
        (2 * i + h, 2 * (i + by) + (1 - h if cross else h)) for i in range(blocks - by) for h in range(2)
    ]
    return lax.ppermute(x, BOTH, pairs)


def body(queries, keys, values, segments):
    h = lax.axis_index("head")
    width = keys.shape[1] // 2

    def columns(x, which):
        return lax.dynamic_slice_in_dim(x, which * width, width, axis=1)

    near = jnp.concatenate([columns(keys, h), columns(values, h)], axis=1)
    cross = jnp.concatenate([columns(keys, 1 - h), columns(values, 1 - h)], axis=1)
    a2 = send(near, 2, False)
    b2 = send(cross, 2, True)
    a1 = send(near, 1, False)
    b1 = send(cross, 1, True)
    b0 = send(cross, 0, True)
    return attention(segments.reshape(-1, HALF), queries, near, b0, a1, b1, a2, b2)


def solution(mesh):
    placed = (P("ctx", "head"), P(("ctx", "head"), None), P(("ctx", "head"), None), P())
    return jax.shard_map(
        body, mesh=mesh, in_specs=placed, out_specs=P("ctx", "head"), check_vma=False
    )
```

time: 94.8 us -> 39.9 us (0.42)
  the two profiles are of different devices: /device:TPU:24 before, /device:TPU:256 now
where the time goes in v1:
time: 39.9 us; the launch traced here: 39.7 us
  starting transfers between devices  16.3 us (41%)
  waiting for transfers between devices  16.1 us (40%)
  Pallas kernels  5.89 us (15%)
  local copies, waits for them, and re-layouts  1.23 us (3%)
    ppermute x5, starting transfers between devices, send(): return lax.ppermute(x, BOTH, pairs)  16.3 us
    ppermute x5, waiting for transfers between devices, send(): return lax.ppermute(x, BOTH, pairs)  16.1 us
    pallas_call x1, Pallas kernels, attention(): pl.pallas_call(attention_kernel, out_shape=jax.ShapeDtypeStruct(q.shape,...  5.89 us
    dynamic_slice x1, local copies, waits for them, and re-layouts, columns(): return lax.dynamic_slice_in_dim(x, which * width, width, axis=1)  1.22 us
  transfers between devices with their start and end apart: 5, of which 4 were waited for; matrix products, arithmetic and copies ran while one was open for 0% of the time, Pallas kernels for 0%

profile of v1, /device:TPU:256, one launch (start us, length us, event | category | flops | bytes accessed | tf_op | source)
XLA Modules:
  0.0 39.7 jit_solution(17571433771705043473)
XLA Ops:
  0.0 0.0 copy-start
  0.0 1.2 %constant_dynamic-slice_fusion = (bf16[128,512]{1,0:T(8,128)(2,1)S(1)}, bf16[128,512]{1,0:T(8,128)(2,1)S(1)}, bf16[128,512]{1,0:T(8,128)(2,1)S(1)}, bf16[128,512]{1,0:T(8,128)(2,1)S(1)}) fusion(bf16[128,1024]{1,0:T(8,128)(2,1)} %param.6, s32[]{:T(128)S(6)} %select_n.9, s32[]{:T(128)S(6)} %select_n.8, bf16[128,1024]{1,0:T(8,128)(2,1)} %param.5), kind=kLoop, calls=%fused_computation.2 | loop fusion | bytes 1048584 | tf_op jit(solution)/shard_map/dynamic_slice | solution.py:93
  1.2 3.4 %collective-permute-start.3 = (bf16[128,1024]{1,0:T(8,128)(2,1)S(1)}, bf16[128,1024]{1,0:T(8,128)(2,1)S(1)}, u32[]{:S(2)}, u32[]{:S(2)}) collective-permute-start(bf16[128,1024]{1,0:T(8,128)(2,1)S(1)} %pad_maximum_fusion.a0), channel_id=1, source_target_pairs={{0,4},{1,5},{2,6},{3,7},{4,8},{5,9},{6,10},{7,11},{8,12},{9,13},{1... | collective-permute-start | bytes 786440 | tf_op jit(solution)/shard_map/ppermute | solution.py:85
  4.7 1.9 %collective-permute-start.1 = (bf16[128,1024]{1,0:T(8,128)(2,1)S(1)}, bf16[128,1024]{1,0:T(8,128)(2,1)S(1)}, u32[]{:S(2)}, u32[]{:S(2)}) collective-permute-start(bf16[128,1024]{1,0:T(8,128)(2,1)S(1)} %pad_maximum_fusion.a0), channel_id=1, source_target_pairs={{0,2},{1,3},{2,4},{3,5},{4,6},{5,7},{6,8},{7,9},{8,10},{9,11},{10,... | collective-permute-start | bytes 786440 | tf_op jit(solution)/shard_map/ppermute | solution.py:85
  6.6 0.0 copy-start.1
  6.6 4.5 %collective-permute-start.4 = (bf16[128,1024]{1,0:T(8,128)(2,1)S(1)}, bf16[128,1024]{1,0:T(8,128)(2,1)S(1)}, u32[]{:S(2)}, u32[]{:S(2)}) collective-permute-start(bf16[128,1024]{1,0:T(8,128)(2,1)S(1)} %pad_maximum_fusion.1), channel_id=1, source_target_pairs={{0,5},{1,4},{2,7},{3,6},{4,9},{5,8},{6,11},{7,10},{8,13},{9,12},{1... | collective-permute-start | bytes 786440 | tf_op jit(solution)/shard_map/ppermute | solution.py:85
  11.2 3.0 %collective-permute-start.2 = (bf16[128,1024]{1,0:T(8,128)(2,1)S(1)}, bf16[128,1024]{1,0:T(8,128)(2,1)S(1)}, u32[]{:S(2)}, u32[]{:S(2)}) collective-permute-start(bf16[128,1024]{1,0:T(8,128)(2,1)S(1)} %pad_maximum_fusion.1), channel_id=1, source_target_pairs={{0,3},{1,2},{2,5},{3,4},{4,7},{5,6},{6,9},{7,8},{8,11},{9,10},{10,... | collective-permute-start | bytes 786440 | tf_op jit(solution)/shard_map/ppermute | solution.py:85
  14.2 3.5 %collective-permute-start = (bf16[128,1024]{1,0:T(8,128)(2,1)S(1)}, bf16[128,1024]{1,0:T(8,128)(2,1)S(1)}, u32[]{:S(2)}, u32[]{:S(2)}) collective-permute-start(bf16[128,1024]{1,0:T(8,128)(2,1)S(1)} %pad_maximum_fusion.1), channel_id=1, source_target_pairs={{0,1},{1,0},{2,3},{3,2},{4,5},{5,4},{6,7},{7,6},{8,9},{9,8},{10,11... | collective-permute-start | bytes 786440 | tf_op jit(solution)/shard_map/ppermute | solution.py:85
  17.7 0.0 collective-permute-done.3.a2
  17.7 0.3 collective-permute-done.1.a1
  18.0 4.4 %collective-permute-done.4.b2 = bf16[128,1024]{1,0:T(8,128)(2,1)S(1)} collective-permute-done((bf16[128,1024]{1,0:T(8,128)(2,1)S(1)}, bf16[128,1024]{1,0:T(8,128)(2,1)S(1)}, u32[]{:S(2)}, u32[]{:S(2)}) %collective-permute-start.4) | collective-permute-done | bytes 262176 | tf_op jit(solution)/shard_map/ppermute | solution.py:85
  22.4 5.6 %collective-permute-done.2.b1 = bf16[128,1024]{1,0:T(8,128)(2,1)S(1)} collective-permute-done((bf16[128,1024]{1,0:T(8,128)(2,1)S(1)}, bf16[128,1024]{1,0:T(8,128)(2,1)S(1)}, u32[]{:S(2)}, u32[]{:S(2)}) %collective-permute-start.2) | collective-permute-done | bytes 262176 | tf_op jit(solution)/shard_map/ppermute | solution.py:85
  28.0 5.8 %collective-permute-done.b0 = bf16[128,1024]{1,0:T(8,128)(2,1)S(1)} collective-permute-done((bf16[128,1024]{1,0:T(8,128)(2,1)S(1)}, bf16[128,1024]{1,0:T(8,128)(2,1)S(1)}, u32[]{:S(2)}, u32[]{:S(2)}) %collective-permute-start) | collective-permute-done | bytes 262176 | tf_op jit(solution)/shard_map/ppermute | solution.py:85
  33.8 0.0 copy-done
  33.8 0.0 copy-done.1
  33.8 5.9 %shard_map.46 = bf16[256,2048]{1,0:T(8,128)(2,1)} custom-call(s32[512,128]{1,0:T(8,128)S(1)} %bitcast.1, bf16[256,2048]{1,0:T(8,128)(2,1)S(1)} %copy-done, bf16[128,1024]{1,0:T(8,128)(2,1)S(1)} %pad_maximum_fusion.a0, bf16[128,1024]{1,0:T(8,128)(2,1)S(1)} %collective-permute-done.b0, bf16[128,1024]{1,0:T(8,128)(2,1)S(1)} %collective-permute-done.1.a1, ...), custom_call_target="tpu_custom_call" | custom-call | tf_op jit(solution)/shard_map/pallas_call | solution.py:70
  (2 shorter events, 0.0 us)
Async XLA Ops:
  0.0 33.8 %copy-start = (bf16[256,2048]{1,0:T(8,128)(2,1)S(1)}, bf16[256,2048]{1,0:T(8,128)(2,1)}, u32[]{:S(2)}) copy-start(bf16[256,2048]{1,0:T(8,128)(2,1)} %q_ref.1) | copy-start | bytes 3145732
  1.2 16.4 %collective-permute-start.3 = (bf16[128,1024]{1,0:T(8,128)(2,1)S(1)}, bf16[128,1024]{1,0:T(8,128)(2,1)S(1)}, u32[]{:S(2)}, u32[]{:S(2)}) collective-permute-start(bf16[128,1024]{1,0:T(8,128)(2,1)S(1)} %pad_maximum_fusion.a0), channel_id=1, source_target_pairs={{0,4},{1,5},{2,6},{3,7},{4,8},{5,9},{6,10},{7,11},{8,12},{9,13},{1... | collective-permute-start | bytes 786440 | tf_op jit(solution)/shard_map/ppermute | solution.py:85
  4.7 13.4 %collective-permute-start.1 = (bf16[128,1024]{1,0:T(8,128)(2,1)S(1)}, bf16[128,1024]{1,0:T(8,128)(2,1)S(1)}, u32[]{:S(2)}, u32[]{:S(2)}) collective-permute-start(bf16[128,1024]{1,0:T(8,128)(2,1)S(1)} %pad_maximum_fusion.a0), channel_id=1, source_target_pairs={{0,2},{1,3},{2,4},{3,5},{4,6},{5,7},{6,8},{7,9},{8,10},{9,11},{10,... | collective-permute-start | bytes 786440 | tf_op jit(solution)/shard_map/ppermute | solution.py:85
  6.6 27.2 %copy-start.1 = (s32[65536]{0:T(1024)S(1)}, s32[65536]{0:T(1024)}, u32[]{:S(2)}) copy-start(s32[65536]{0:T(1024)} %param.7) | copy-start | bytes 786436
  6.6 15.8 %collective-permute-start.4 = (bf16[128,1024]{1,0:T(8,128)(2,1)S(1)}, bf16[128,1024]{1,0:T(8,128)(2,1)S(1)}, u32[]{:S(2)}, u32[]{:S(2)}) collective-permute-start(bf16[128,1024]{1,0:T(8,128)(2,1)S(1)} %pad_maximum_fusion.1), channel_id=1, source_target_pairs={{0,5},{1,4},{2,7},{3,6},{4,9},{5,8},{6,11},{7,10},{8,13},{9,12},{1... | collective-permute-start | bytes 786440 | tf_op jit(solution)/shard_map/ppermute | solution.py:85
  11.2 16.9 %collective-permute-start.2 = (bf16[128,1024]{1,0:T(8,128)(2,1)S(1)}, bf16[128,1024]{1,0:T(8,128)(2,1)S(1)}, u32[]{:S(2)}, u32[]{:S(2)}) collective-permute-start(bf16[128,1024]{1,0:T(8,128)(2,1)S(1)} %pad_maximum_fusion.1), channel_id=1, source_target_pairs={{0,3},{1,2},{2,5},{3,4},{4,7},{5,6},{6,9},{7,8},{8,11},{9,10},{10,... | collective-permute-start | bytes 786440 | tf_op jit(solution)/shard_map/ppermute | solution.py:85
  14.2 19.7 %collective-permute-start = (bf16[128,1024]{1,0:T(8,128)(2,1)S(1)}, bf16[128,1024]{1,0:T(8,128)(2,1)S(1)}, u32[]{:S(2)}, u32[]{:S(2)}) collective-permute-start(bf16[128,1024]{1,0:T(8,128)(2,1)S(1)} %pad_maximum_fusion.1), channel_id=1, source_target_pairs={{0,1},{1,0},{2,3},{3,2},{4,5},{5,4},{6,7},{7,6},{8,9},{9,8},{10,11... | collective-permute-start | bytes 786440 | tf_op jit(solution)/shard_map/ppermute | solution.py:85

commit v2 on v1

v2 whole, which is shorter than its diff:
```python
import math
import jax
import jax.numpy as jnp
from jax import lax
from jax.experimental import pallas as pl
from jax.experimental.pallas import tpu as pltpu
from jax.sharding import PartitionSpec as P

HD = 128
HALF = 128
BLOCK = 2 * HALF
KV = 4
BOTH = ("ctx", "head")
EXP2_SCALE = HD ** (-0.5) * math.log2(math.e)
VMEM = pl.BlockSpec(memory_space=pltpu.VMEM)
STATE = (jax.ShapeDtypeStruct((2 * KV, 4 * HALF, HD), jnp.float32),) * 3
BIAS = jax.ShapeDtypeStruct((2, HALF, 6 * HALF), jnp.float32)


def is_first():
    return lax.axis_index("head") == 0


def is_even():
    return lax.rem(lax.axis_index("ctx"), 2) == 0


def put_masks(seg_ref, bias_ref):
    c = lax.axis_index("ctx")
    row = lax.broadcasted_iota(jnp.int32, (HALF, HALF), 0)
    col = lax.broadcasted_iota(jnp.int32, (HALF, HALF), 1)
    for qb in range(2):
        q_seg = jnp.broadcast_to(seg_ref[pl.ds(2 * c + qb, 1), :], (HALF, HALF)).T
        for t in range(6):
            key_half = 2 * c - 4 + t
            k_seg = seg_ref[pl.ds(jnp.maximum(key_half, 0), 1), :]
            ok = (q_seg == k_seg) & (key_half >= 0)
            if t == qb + 4:
                ok = ok & (col <= row)
            if t == qb:
                ok = ok & (col > row)
            if t - qb not in range(5):
                ok = jnp.zeros_like(ok)
            bias_ref[qb, :, t * HALF : (t + 1) * HALF] = jnp.where(ok, 0.0, -jnp.inf)


def fold(q_ref, g, qb, k, v, bias, old, new):
    group = q_ref.shape[1] // (KV * HD)
    at, count = KV * qb + g, k.shape[0]
    q = jnp.concatenate(
        [
            q_ref[qb * HALF : (qb + 1) * HALF, (g * group + r) * HD : (g * group + r + 1) * HD]
            for r in range(group)
        ],
        axis=0,
    )
    s = lax.dot_general(q, k, (((1,), (1,)), ((), ())), preferred_element_type=jnp.float32)
    s = (s.reshape(group, HALF, count) + bias[None]).reshape(group * HALF, count)
    before = jnp.full((group * HALF, HD), -1e30, jnp.float32) if old is None else old[0][at]
    top = jnp.maximum(before, jnp.max(s, axis=-1, keepdims=True))
    p = jnp.exp2((s - jnp.concatenate([top] * (count // HD), axis=1)) * EXP2_SCALE).astype(jnp.bfloat16)
    v = jnp.concatenate([v, jnp.ones_like(v)], axis=1)
    o = jnp.dot(p, v, preferred_element_type=jnp.float32)
    acc, total = o[:, :HD], o[:, HD:]
    if old is not None:
        keep = jnp.exp2((before - top) * EXP2_SCALE)
        acc = acc + old[1][at] * keep
        total = total + old[2][at] * keep
    if new is not None:
        new[0][at], new[1][at], new[2][at] = top, acc, total
    return acc, total


def head_of(ref, at):
    return ref[:, at * HD : (at + 1) * HD]


def halves(first, near, cross):
    return [jnp.where(first, near, cross), jnp.where(first, cross, near)]


def half_bias(bias_ref, qb, t):
    return bias_ref[qb, :, t * HALF : (t + 1) * HALF]


def near_kernel(seg_ref, q_ref, x1, x2, bias_ref, *new):
    put_masks(seg_ref, bias_ref)
    first, even = is_first(), is_even()
    for g in range(KV):
        k, v = (jnp.where(even, head_of(x2, at), head_of(x1, at)) for at in (g, KV + g))
        for qb in range(2):
            bias = jnp.where(first, half_bias(bias_ref, qb, 4), half_bias(bias_ref, qb, 5))
            fold(q_ref, g, qb, k, v, bias, None, new)


def cross_bias(first, bias_ref, qb):
    return jnp.where(first, half_bias(bias_ref, qb, 5), half_bias(bias_ref, qb, 4))


def even_own_kernel(q_ref, bias_ref, x2, r1, *new):
    first = is_first()

    @pl.when(is_even())
    def _():
        for g in range(KV):
            k, v = (jnp.concatenate(halves(first, head_of(x2, at), head_of(r1, at)), axis=0) for at in (g, KV + g))
            for qb in range(2):
                seen = HALF * (qb + 1)
                fold(q_ref, g, qb, k[:seen], v[:seen], bias_ref[qb, :, 2 * BLOCK : 2 * BLOCK + seen], None, new)


def previous_kernel(q_ref, bias_ref, near_pair, cross_pair, *state):
    first, even = is_first(), is_even()
    new = state[6:]

    def step(at_core, old):
        for g in range(KV):
            k, v = (
                jnp.concatenate(halves(first, *(head_of(x, at)[at_core] for x in (near_pair, cross_pair))), axis=0)
                for at in (g, KV + g)
            )
            for qb in range(2):
                fold(q_ref, g, qb, k, v, bias_ref[qb, :, BLOCK : 2 * BLOCK], old, new)

    @pl.when(even)
    def _():
        step(slice(HALF, BLOCK), state[3:6])

    @pl.when(jnp.logical_not(even))
    def _():
        step(slice(0, HALF), state[:3])


def last_kernel(q_ref, bias_ref, r1, r2, r3, r4, *rest):
    old, (out_ref, rows_ref, sems) = rest[:3], rest[3:]
    first, even = is_first(), is_even()
    group = q_ref.shape[1] // (KV * HD)

    def finish(near, cross, own):
        copies = []
        for g in range(KV):
            kv = []
            for at in (g, KV + g):
                parts = halves(first, head_of(near, at), head_of(cross, at))
                kv.append(jnp.concatenate(parts if own is None else parts + [head_of(own, at)], axis=0))
            for qb in range(2):
                k, v = (x[qb * HALF :] for x in kv)
                bias = bias_ref[qb, :, qb * HALF : BLOCK]
                if own is not None:
                    bias = jnp.concatenate([bias, cross_bias(first, bias_ref, qb)], axis=1)
                acc, total = fold(q_ref, g, qb, k, v, bias, old, None)
                guess = pl.reciprocal(total, approx=True)
                res = (acc * (guess * (2.0 - total * guess))).astype(jnp.bfloat16)
                for r in range(group):
                    cols = slice((g * group + r) * HD, (g * group + r + 1) * HD)
                    rows_ref[qb * HALF : (qb + 1) * HALF, cols] = res[r * HALF : (r + 1) * HALF]
            cols = pl.ds(g * group * HD, group * HD)
            copies.append(pltpu.make_async_copy(rows_ref.at[:, cols], out_ref.at[:, cols], sems.at[g]))
            copies[-1].start()
        for copy in copies:
            copy.wait()

    @pl.when(even)
    def _():
        finish(r3, r4, None)

    @pl.when(jnp.logical_not(even))
    def _():
        finish(r1, r2, r3)


def call(kernel, outs, *args, out_specs=None, scratch=()):
    return pl.pallas_call(
        kernel,
        out_shape=outs,
        in_specs=[VMEM] * len(args),
        out_specs=jax.tree.map(lambda _: VMEM, outs) if out_specs is None else out_specs,
        scratch_shapes=scratch,
        compiler_params=pltpu.CompilerParams(vmem_limit_bytes=24 * 1024 * 1024),
    )(*args)


def call_last(queries, *args):
    return call(
        last_kernel,
        jax.ShapeDtypeStruct(queries.shape, queries.dtype),
        queries,
        *args,
        out_specs=pl.BlockSpec(memory_space=pl.ANY),
        scratch=[pltpu.VMEM(queries.shape, queries.dtype), pltpu.SemaphoreType.DMA((KV,))],
    )


def send(x, odd, even):
    blocks = lax.axis_size("ctx")
    pairs = []
    for i in range(blocks):
        move = odd if i % 2 else even
        if move is not None and i + move[0] < blocks:
            pairs += [(2 * i + h, 2 * (i + move[0]) + (1 - h if move[1] else h)) for h in range(2)]
    return lax.ppermute(x, BOTH, pairs)


def core_pair(x):
    blocks = lax.axis_size("ctx")
    return lax.all_gather(x, "ctx", axis=0, tiled=True, axis_index_groups=[[i, i + 1] for i in range(0, blocks, 2)])


def body(queries, keys, values, segments):
    h = lax.axis_index("head")
    width = keys.shape[1] // 2

    def columns(x, which):
        return lax.dynamic_slice_in_dim(x, which * width, width, axis=1)

    even = is_even()
    which = jnp.where(even, 1 - h, h)
    x1 = jnp.concatenate([columns(keys, which), columns(values, which)], axis=1)
    x2 = jnp.concatenate([columns(keys, 1 - which), columns(values, 1 - which)], axis=1)
    r1 = send(x1, odd=(2, False), even=(0, True))
    r2 = send(x2, odd=(2, True), even=None)
    bias, *state = call(near_kernel, (BIAS,) + STATE, segments.reshape(-1, HALF), queries, x1, x2)
    x1_later, x2_later, bias = lax.optimization_barrier((x1, x2, bias))
    r3 = send(x2_later, odd=(0, True), even=(2, False))
    r4 = send(x1_later, odd=None, even=(2, True))
    even_state = call(even_own_kernel, STATE, queries, bias, x2, r1)
    r1_later, *even_state = lax.optimization_barrier((r1, *even_state))
    near_pair = core_pair(jnp.where(even, x2, r1_later))
    r2_later, near_pair = lax.optimization_barrier((r2, near_pair))
    cross_pair = core_pair(jnp.where(even, r1, r2_later))
    state = call(previous_kernel, STATE, queries, bias, near_pair, cross_pair, *state, *even_state)
    return call_last(queries, bias, r1, r2, r3, r4, *state)


def solution(mesh):
    placed = (P("ctx", "head"), P(("ctx", "head"), None), P(("ctx", "head"), None), P())
    return jax.shard_map(
        body, mesh=mesh, in_specs=placed, out_specs=P("ctx", "head"), check_vma=False
    )
```

time: 39.9 us -> 30.8 us (0.77)
  the two profiles are of different devices: /device:TPU:256 before, /device:TPU:24 now
where the time goes in v2:
time: 30.8 us; the launch traced here: 30.5 us
  starting transfers between devices  10.9 us (35%)
  blocking collectives  8.11 us (26%)
  Pallas kernels  8.06 us (26%)
  waiting for transfers between devices  1.97 us (6%)
  local copies, waits for them, and re-layouts  1.24 us (4%)
    ppermute x4, starting transfers between devices, send(): return lax.ppermute(x, BOTH, pairs)  10.9 us
    all_gather x2, blocking collectives, core_pair(): lax.all_gather(x, 'ctx', axis=0, tiled=True, axis_index_groups=[[i, i + 1...  8.11 us
    pallas_call x4, Pallas kernels, call(): pl.pallas_call(kernel, out_shape=outs, in_specs=[VMEM] * len(args), out_s...  8.06 us
    ppermute x4, waiting for transfers between devices, send(): return lax.ppermute(x, BOTH, pairs)  1.97 us
    dynamic_slice x1, local copies, waits for them, and re-layouts, columns(): return lax.dynamic_slice_in_dim(x, which * width, width, axis=1)  1.23 us
  transfers between devices with their start and end apart: 4, of which 1 were waited for; matrix products, arithmetic and copies ran while one was open for 0% of the time, Pallas kernels for 18%

profile of v2, /device:TPU:24, one launch (start us, length us, event | category | flops | bytes accessed | tf_op | source)
XLA Modules:
  0.0 30.5 jit_solution(5713299981454436712)
XLA Ops:
  0.0 0.0 copy-start
  0.0 0.0 copy-start.1
  0.0 1.2 %constant_dynamic-slice_fusion = (bf16[128,512]{1,0:T(8,128)(2,1)S(1)}, bf16[128,512]{1,0:T(8,128)(2,1)S(1)}, bf16[128,512]{1,0:T(8,128)(2,1)S(1)}, bf16[128,512]{1,0:T(8,128)(2,1)S(1)}) fusion(bf16[128,1024]{1,0:T(8,128)(2,1)} %param.6, s32[]{:T(128)S(6)} %select_n.26, s32[]{:T(128)S(6)} %select_n.25, bf16[128,1024]{1,0:T(8,128)(2,1)} %param.5), kind=kLoop, calls=%fused_computation.4 | loop fusion | bytes 1048584 | tf_op jit(solution)/shard_map/dynamic_slice | solution.py:214
  1.3 2.7 %collective-permute-start = (bf16[128,1024]{1,0:T(8,128)(2,1)S(1)}, bf16[128,1024]{1,0:T(8,128)(2,1)S(1)}, u32[]{:S(2)}, u32[]{:S(2)}) collective-permute-start(bf16[128,1024]{1,0:T(8,128)(2,1)S(1)} %pad_maximum_fusion.x1), channel_id=1, source_target_pairs={{0,1},{1,0},{2,6},{3,7},{4,5},{5,4},{6,10},{7,11},{8,9},{9,8},{10,... | collective-permute-start | bytes 786440 | tf_op jit(solution)/shard_map/ppermute | solution.py:201
  4.0 0.7 %collective-permute-start.1 = (bf16[128,1024]{1,0:T(8,128)(2,1)S(1)}, bf16[128,1024]{1,0:T(8,128)(2,1)S(1)}, u32[]{:S(2)}, u32[]{:S(2)}) collective-permute-start(bf16[128,1024]{1,0:T(8,128)(2,1)S(1)} %pad_maximum_fusion.1.x2), channel_id=1, source_target_pairs={{2,7},{3,6},{6,11},{7,10},{10,15},{11,14},{14,19},{15,18},{18,23},... | collective-permute-start | bytes 786440 | tf_op jit(solution)/shard_map/ppermute | solution.py:201
  4.6 0.0 copy-done
  4.6 0.0 copy-done.1
  4.7 1.9 %shard_map.46 = (f32[2,128,768]{2,1,0:T(8,128)S(1)}, f32[8,512,128]{2,1,0:T(8,128)S(1)}, f32[8,512,128]{2,1,0:T(8,128)S(1)}, f32[8,512,128]{2,1,0:T(8,128)S(1)}) custom-call(s32[512,128]{1,0:T(8,128)S(1)} %bitcast.1, bf16[256,2048]{1,0:T(8,128)(2,1)S(1)} %copy-done, bf16[128,1024]{1,0:T(8,128)(2,1)S(1)} %pad_maximum_fusion.x1, ...), custom_call_target="tpu_custom_call" | custom-call | tf_op jit(solution)/shard_map/pallas_call | solution.py:173
  6.6 3.4 %collective-permute-start.2 = (bf16[128,1024]{1,0:T(8,128)(2,1)S(1)}, bf16[128,1024]{1,0:T(8,128)(2,1)S(1)}, u32[]{:S(2)}, u32[]{:S(2)}) collective-permute-start(bf16[128,1024]{1,0:T(8,128)(2,1)S(1)} %pad_maximum_fusion.1.x2), channel_id=1, source_target_pairs={{0,4},{1,5},{2,3},{3,2},{4,8},{5,9},{6,7},{7,6},{8,12},{9,13},{10,... | collective-permute-start | bytes 786440 | tf_op jit(solution)/shard_map/ppermute | solution.py:201
  10.0 4.1 %collective-permute-start.3 = (bf16[128,1024]{1,0:T(8,128)(2,1)S(1)}, bf16[128,1024]{1,0:T(8,128)(2,1)S(1)}, u32[]{:S(2)}, u32[]{:S(2)}) collective-permute-start(bf16[128,1024]{1,0:T(8,128)(2,1)S(1)} %pad_maximum_fusion.x1), channel_id=1, source_target_pairs={{0,5},{1,4},{4,9},{5,8},{8,13},{9,12},{12,17},{13,16},{16,21},{17,... | collective-permute-start | bytes 786440 | tf_op jit(solution)/shard_map/ppermute | solution.py:201
  14.1 0.0 collective-permute-done.r1
  14.1 1.8 %shard_map.47 = (f32[8,512,128]{2,1,0:T(8,128)S(1)}, f32[8,512,128]{2,1,0:T(8,128)S(1)}, f32[8,512,128]{2,1,0:T(8,128)S(1)}) custom-call(bf16[256,2048]{1,0:T(8,128)(2,1)S(1)} %copy-done, f32[2,128,768]{2,1,0:T(8,128)S(1)} %get-tuple-element.25.bias_ref, bf16[128,1024]{1,0:T(8,128)(2,1)S(1)} %pad_maximum_fusion.1.x2, ...), custom_call_target="tpu_custom_call" | custom-call | tf_op jit(solution)/shard_map/pallas_call | solution.py:173
  15.9 0.1 broadcast_select_fusion.1
  15.9 5.9 %all_gather.6.near_pair = bf16[256,1024]{1,0:T(8,128)(2,1)S(1)} all-gather(bf16[128,1024]{1,0:T(8,128)(2,1)S(1)} %broadcast_select_fusion.1), channel_id=1, replica_groups={{0,2},{4,6},{8,10},{12,14},{16,18},{20,22},{24,26},{28,30},{32,34},{36,..., dimensions={0}, use_global_device_ids=true | all-gather | bytes 786432 | tf_op jit(solution)/shard_map/all_gather | solution.py:206
  21.9 0.0 collective-permute-done.1.r2
  21.9 2.2 %all_gather.7.cross_pair = bf16[256,1024]{1,0:T(8,128)(2,1)S(1)} all-gather(bf16[128,1024]{1,0:T(8,128)(2,1)S(1)} %broadcast_select_fusion), channel_id=1, replica_groups={{0,2},{4,6},{8,10},{12,14},{16,18},{20,22},{24,26},{28,30},{32,34},{36,..., dimensions={0}, use_global_device_ids=true | all-gather | bytes 786432 | tf_op jit(solution)/shard_map/all_gather | solution.py:206
  24.1 1.7 %shard_map.48 = (f32[8,512,128]{2,1,0:T(8,128)S(1)}, f32[8,512,128]{2,1,0:T(8,128)S(1)}, f32[8,512,128]{2,1,0:T(8,128)S(1)}) custom-call(bf16[256,2048]{1,0:T(8,128)(2,1)S(1)} %copy-done, f32[2,128,768]{2,1,0:T(8,128)S(1)} %get-tuple-element.25.bias_ref, bf16[256,1024]{1,0:T(8,128)(2,1)S(1)} %all_gather.6.near_pair, ...), custom_call_target="tpu_custom_call" | custom-call | tf_op jit(solution)/shard_map/pallas_call | solution.py:173
  25.8 0.0 collective-permute-done.2.r3
  25.8 2.0 %collective-permute-done.3.r4 = bf16[128,1024]{1,0:T(8,128)(2,1)S(1)} collective-permute-done((bf16[128,1024]{1,0:T(8,128)(2,1)S(1)}, bf16[128,1024]{1,0:T(8,128)(2,1)S(1)}, u32[]{:S(2)}, u32[]{:S(2)}) %collective-permute-start.3) | collective-permute-done | bytes 262176 | tf_op jit(solution)/shard_map/ppermute | solution.py:201
  27.8 2.7 %shard_map.49 = bf16[256,2048]{1,0:T(8,128)(2,1)} custom-call(bf16[256,2048]{1,0:T(8,128)(2,1)S(1)} %copy-done, f32[2,128,768]{2,1,0:T(8,128)S(1)} %get-tuple-element.25.bias_ref, bf16[128,1024]{1,0:T(8,128)(2,1)S(1)} %collective-permute-done.r1, bf16[128,1024]{1,0:T(8,128)(2,1)S(1)} %collective-permute-done.1.r2, ...), custom_call_target="tpu_custom_call" | custom-call | tf_op jit(solution)/shard_map/pallas_call | solution.py:173
  (3 shorter events, 0.1 us)
Async XLA Ops:
  0.0 4.6 %copy-start = (bf16[256,2048]{1,0:T(8,128)(2,1)S(1)}, bf16[256,2048]{1,0:T(8,128)(2,1)}, u32[]{:S(2)}) copy-start(bf16[256,2048]{1,0:T(8,128)(2,1)} %q_ref.7) | copy-start | bytes 3145732
  0.0 4.6 %copy-start.1 = (s32[65536]{0:T(1024)S(1)}, s32[65536]{0:T(1024)}, u32[]{:S(2)}) copy-start(s32[65536]{0:T(1024)} %param.7) | copy-start | bytes 786436
  1.3 12.8 %collective-permute-start = (bf16[128,1024]{1,0:T(8,128)(2,1)S(1)}, bf16[128,1024]{1,0:T(8,128)(2,1)S(1)}, u32[]{:S(2)}, u32[]{:S(2)}) collective-permute-start(bf16[128,1024]{1,0:T(8,128)(2,1)S(1)} %pad_maximum_fusion.x1), channel_id=1, source_target_pairs={{0,1},{1,0},{2,6},{3,7},{4,5},{5,4},{6,10},{7,11},{8,9},{9,8},{10,... | collective-permute-start | bytes 786440 | tf_op jit(solution)/shard_map/ppermute | solution.py:201
  4.0 17.9 %collective-permute-start.1 = (bf16[128,1024]{1,0:T(8,128)(2,1)S(1)}, bf16[128,1024]{1,0:T(8,128)(2,1)S(1)}, u32[]{:S(2)}, u32[]{:S(2)}) collective-permute-start(bf16[128,1024]{1,0:T(8,128)(2,1)S(1)} %pad_maximum_fusion.1.x2), channel_id=1, source_target_pairs={{2,7},{3,6},{6,11},{7,10},{10,15},{11,14},{14,19},{15,18},{18,23},... | collective-permute-start | bytes 786440 | tf_op jit(solution)/shard_map/ppermute | solution.py:201
  6.6 19.3 %collective-permute-start.2 = (bf16[128,1024]{1,0:T(8,128)(2,1)S(1)}, bf16[128,1024]{1,0:T(8,128)(2,1)S(1)}, u32[]{:S(2)}, u32[]{:S(2)}) collective-permute-start(bf16[128,1024]{1,0:T(8,128)(2,1)S(1)} %pad_maximum_fusion.1.x2), channel_id=1, source_target_pairs={{0,4},{1,5},{2,3},{3,2},{4,8},{5,9},{6,7},{7,6},{8,12},{9,13},{10,... | collective-permute-start | bytes 786440 | tf_op jit(solution)/shard_map/ppermute | solution.py:201
  10.0 17.8 %collective-permute-start.3 = (bf16[128,1024]{1,0:T(8,128)(2,1)S(1)}, bf16[128,1024]{1,0:T(8,128)(2,1)S(1)}, u32[]{:S(2)}, u32[]{:S(2)}) collective-permute-start(bf16[128,1024]{1,0:T(8,128)(2,1)S(1)} %pad_maximum_fusion.x1), channel_id=1, source_target_pairs={{0,5},{1,4},{4,9},{5,8},{8,13},{9,12},{12,17},{13,16},{16,21},{17,... | collective-permute-start | bytes 786440 | tf_op jit(solution)/shard_map/ppermute | solution.py:201

commit v3 on v2

--- a/solution.py
+++ b/solution.py
@@ -1,3 +1,4 @@
+import functools
 import math
 import jax
 import jax.numpy as jnp
@@ -10,6 +11,7 @@
 HALF = 128
 BLOCK = 2 * HALF
 KV = 4
+FAR = 64.0
 BOTH = ("ctx", "head")
 EXP2_SCALE = HD ** (-0.5) * math.log2(math.e)
 VMEM = pl.BlockSpec(memory_space=pltpu.VMEM)
@@ -71,6 +73,26 @@
     return acc, total
 
 
+def fold_unmoved(q_ref, g, qb, k, v, bias, old):
+    group = q_ref.shape[1] // (KV * HD)
+    at, count = KV * qb + g, k.shape[0]
+    q = jnp.concatenate(
+        [
+            q_ref[qb * HALF : (qb + 1) * HALF, (g * group + r) * HD : (g * group + r + 1) * HD]
+            for r in range(group)
+        ],
+        axis=0,
+    )
+    s = lax.dot_general(q, k, (((1,), (1,)), ((), ())), preferred_element_type=jnp.float32)
+    s = (s.reshape(group, HALF, count) + bias[None]).reshape(group * HALF, count)
+    above = (s - jnp.concatenate([old[0][at]] * (count // HD), axis=1)) * EXP2_SCALE
+    v = jnp.concatenate([v, jnp.ones_like(v)], axis=1)
+    o = jnp.dot(jnp.exp2(above).astype(jnp.bfloat16), v, preferred_element_type=jnp.float32)
+    highest = functools.reduce(jnp.maximum, [above[:, n * HD : (n + 1) * HD] for n in range(count // HD)])
+    highest = jnp.max(highest.reshape(-1, 8, HD), axis=0)
+    return o[:, :HD] + old[1][at], o[:, HD:] + old[2][at], highest
+
+
 def head_of(ref, at):
     return ref[:, at * HD : (at + 1) * HD]
 
@@ -136,8 +158,8 @@
     first, even = is_first(), is_even()
     group = q_ref.shape[1] // (KV * HD)
 
-    def finish(near, cross, own):
-        copies = []
+    def finish(near, cross, own, unmoved):
+        copies, highest = [], None
         for g in range(KV):
             kv = []
             for at in (g, KV + g):
@@ -148,25 +170,34 @@
                 bias = bias_ref[qb, :, qb * HALF : BLOCK]
                 if own is not None:
                     bias = jnp.concatenate([bias, cross_bias(first, bias_ref, qb)], axis=1)
-                acc, total = fold(q_ref, g, qb, k, v, bias, old, None)
-                guess = pl.reciprocal(total, approx=True)
-                res = (acc * (guess * (2.0 - total * guess))).astype(jnp.bfloat16)
+                if unmoved:
+                    acc, total, high = fold_unmoved(q_ref, g, qb, k, v, bias, old)
+                    highest = high if highest is None else jnp.maximum(highest, high)
+                else:
+                    acc, total = fold(q_ref, g, qb, k, v, bias, old, None)
+                res = (acc * pltpu.reciprocal(total, approx=True)).astype(jnp.bfloat16)
                 for r in range(group):
                     cols = slice((g * group + r) * HD, (g * group + r + 1) * HD)
                     rows_ref[qb * HALF : (qb + 1) * HALF, cols] = res[r * HALF : (r + 1) * HALF]
             cols = pl.ds(g * group * HD, group * HD)
             copies.append(pltpu.make_async_copy(rows_ref.at[:, cols], out_ref.at[:, cols], sems.at[g]))
             copies[-1].start()
+        far = jnp.logical_not(jnp.max(highest) <= FAR) if unmoved else None
         for copy in copies:
             copy.wait()
+        return far
 
     @pl.when(even)
     def _():
-        finish(r3, r4, None)
+        far = finish(r3, r4, None, True)
+
+        @pl.when(far)
+        def _():
+            finish(r3, r4, None, False)
 
     @pl.when(jnp.logical_not(even))
     def _():
-        finish(r1, r2, r3)
+        finish(r1, r2, r3, False)
 
 
 def call(kernel, outs, *args, out_specs=None, scratch=()):

time: 30.8 us -> 30.3 us (0.984)
  Pallas kernels: 8.06 us -> 7.59 us
    pallas_call x4, Pallas kernels: 8.06 us -> 7.59 us  [call(): pl.pallas_call(kernel, out_shape=outs, in_specs=[VMEM] * len(args), out_s...]
where the time goes in v3:
time: 30.3 us; the launch traced here: 30 us
  starting transfers between devices  10.9 us (36%)
  blocking collectives  8.11 us (27%)
  Pallas kernels  7.59 us (25%)
  waiting for transfers between devices  1.97 us (7%)
  local copies, waits for them, and re-layouts  1.24 us (4%)
    ppermute x4, starting transfers between devices, send(): return lax.ppermute(x, BOTH, pairs)  10.9 us
    all_gather x2, blocking collectives, core_pair(): lax.all_gather(x, 'ctx', axis=0, tiled=True, axis_index_groups=[[i, i + 1...  8.11 us
    pallas_call x4, Pallas kernels, call(): pl.pallas_call(kernel, out_shape=outs, in_specs=[VMEM] * len(args), out_s...  7.59 us
    ppermute x4, waiting for transfers between devices, send(): return lax.ppermute(x, BOTH, pairs)  1.97 us
    dynamic_slice x1, local copies, waits for them, and re-layouts, columns(): return lax.dynamic_slice_in_dim(x, which * width, width, axis=1)  1.23 us
  transfers between devices with their start and end apart: 4, of which 1 were waited for; matrix products, arithmetic and copies ran while one was open for 0% of the time, Pallas kernels for 18%

profile of v3, /device:TPU:24, one launch (start us, length us, event | category | flops | bytes accessed | tf_op | source)
XLA Modules:
  0.0 30.0 jit_solution(367367555595129173)
XLA Ops:
  0.0 0.0 copy-start
  0.0 0.0 copy-start.1
  0.0 1.2 %constant_dynamic-slice_fusion = (bf16[128,512]{1,0:T(8,128)(2,1)S(1)}, bf16[128,512]{1,0:T(8,128)(2,1)S(1)}, bf16[128,512]{1,0:T(8,128)(2,1)S(1)}, bf16[128,512]{1,0:T(8,128)(2,1)S(1)}) fusion(bf16[128,1024]{1,0:T(8,128)(2,1)} %param.6, s32[]{:T(128)S(6)} %select_n.26, s32[]{:T(128)S(6)} %select_n.25, bf16[128,1024]{1,0:T(8,128)(2,1)} %param.5), kind=kLoop, calls=%fused_computation.4 | loop fusion | bytes 1048584 | tf_op jit(solution)/shard_map/dynamic_slice | solution.py:245
  1.3 2.7 %collective-permute-start = (bf16[128,1024]{1,0:T(8,128)(2,1)S(1)}, bf16[128,1024]{1,0:T(8,128)(2,1)S(1)}, u32[]{:S(2)}, u32[]{:S(2)}) collective-permute-start(bf16[128,1024]{1,0:T(8,128)(2,1)S(1)} %pad_maximum_fusion.x1), channel_id=1, source_target_pairs={{0,1},{1,0},{2,6},{3,7},{4,5},{5,4},{6,10},{7,11},{8,9},{9,8},{10,... | collective-permute-start | bytes 786440 | tf_op jit(solution)/shard_map/ppermute | solution.py:232
  4.0 0.7 %collective-permute-start.1 = (bf16[128,1024]{1,0:T(8,128)(2,1)S(1)}, bf16[128,1024]{1,0:T(8,128)(2,1)S(1)}, u32[]{:S(2)}, u32[]{:S(2)}) collective-permute-start(bf16[128,1024]{1,0:T(8,128)(2,1)S(1)} %pad_maximum_fusion.1.x2), channel_id=1, source_target_pairs={{2,7},{3,6},{6,11},{7,10},{10,15},{11,14},{14,19},{15,18},{18,23},... | collective-permute-start | bytes 786440 | tf_op jit(solution)/shard_map/ppermute | solution.py:232
  4.6 0.0 copy-done
  4.6 0.0 copy-done.1
  4.7 1.9 %shard_map.46 = (f32[2,128,768]{2,1,0:T(8,128)S(1)}, f32[8,512,128]{2,1,0:T(8,128)S(1)}, f32[8,512,128]{2,1,0:T(8,128)S(1)}, f32[8,512,128]{2,1,0:T(8,128)S(1)}) custom-call(s32[512,128]{1,0:T(8,128)S(1)} %bitcast.1, bf16[256,2048]{1,0:T(8,128)(2,1)S(1)} %copy-done, bf16[128,1024]{1,0:T(8,128)(2,1)S(1)} %pad_maximum_fusion.x1, ...), custom_call_target="tpu_custom_call" | custom-call | tf_op jit(solution)/shard_map/pallas_call | solution.py:204
  6.6 3.4 %collective-permute-start.2 = (bf16[128,1024]{1,0:T(8,128)(2,1)S(1)}, bf16[128,1024]{1,0:T(8,128)(2,1)S(1)}, u32[]{:S(2)}, u32[]{:S(2)}) collective-permute-start(bf16[128,1024]{1,0:T(8,128)(2,1)S(1)} %pad_maximum_fusion.1.x2), channel_id=1, source_target_pairs={{0,4},{1,5},{2,3},{3,2},{4,8},{5,9},{6,7},{7,6},{8,12},{9,13},{10,... | collective-permute-start | bytes 786440 | tf_op jit(solution)/shard_map/ppermute | solution.py:232
  10.0 4.1 %collective-permute-start.3 = (bf16[128,1024]{1,0:T(8,128)(2,1)S(1)}, bf16[128,1024]{1,0:T(8,128)(2,1)S(1)}, u32[]{:S(2)}, u32[]{:S(2)}) collective-permute-start(bf16[128,1024]{1,0:T(8,128)(2,1)S(1)} %pad_maximum_fusion.x1), channel_id=1, source_target_pairs={{0,5},{1,4},{4,9},{5,8},{8,13},{9,12},{12,17},{13,16},{16,21},{17,... | collective-permute-start | bytes 786440 | tf_op jit(solution)/shard_map/ppermute | solution.py:232
  14.1 0.0 collective-permute-done.r1
  14.1 1.8 %shard_map.47 = (f32[8,512,128]{2,1,0:T(8,128)S(1)}, f32[8,512,128]{2,1,0:T(8,128)S(1)}, f32[8,512,128]{2,1,0:T(8,128)S(1)}) custom-call(bf16[256,2048]{1,0:T(8,128)(2,1)S(1)} %copy-done, f32[2,128,768]{2,1,0:T(8,128)S(1)} %get-tuple-element.25.bias_ref, bf16[128,1024]{1,0:T(8,128)(2,1)S(1)} %pad_maximum_fusion.1.x2, ...), custom_call_target="tpu_custom_call" | custom-call | tf_op jit(solution)/shard_map/pallas_call | solution.py:204
  15.9 0.1 broadcast_select_fusion.1
  15.9 5.9 %all_gather.6.near_pair = bf16[256,1024]{1,0:T(8,128)(2,1)S(1)} all-gather(bf16[128,1024]{1,0:T(8,128)(2,1)S(1)} %broadcast_select_fusion.1), channel_id=1, replica_groups={{0,2},{4,6},{8,10},{12,14},{16,18},{20,22},{24,26},{28,30},{32,34},{36,..., dimensions={0}, use_global_device_ids=true | all-gather | bytes 786432 | tf_op jit(solution)/shard_map/all_gather | solution.py:237
  21.9 0.0 collective-permute-done.1.r2
  21.9 2.2 %all_gather.7.cross_pair = bf16[256,1024]{1,0:T(8,128)(2,1)S(1)} all-gather(bf16[128,1024]{1,0:T(8,128)(2,1)S(1)} %broadcast_select_fusion), channel_id=1, replica_groups={{0,2},{4,6},{8,10},{12,14},{16,18},{20,22},{24,26},{28,30},{32,34},{36,..., dimensions={0}, use_global_device_ids=true | all-gather | bytes 786432 | tf_op jit(solution)/shard_map/all_gather | solution.py:237
  24.1 1.7 %shard_map.48 = (f32[8,512,128]{2,1,0:T(8,128)S(1)}, f32[8,512,128]{2,1,0:T(8,128)S(1)}, f32[8,512,128]{2,1,0:T(8,128)S(1)}) custom-call(bf16[256,2048]{1,0:T(8,128)(2,1)S(1)} %copy-done, f32[2,128,768]{2,1,0:T(8,128)S(1)} %get-tuple-element.25.bias_ref, bf16[256,1024]{1,0:T(8,128)(2,1)S(1)} %all_gather.6.near_pair, ...), custom_call_target="tpu_custom_call" | custom-call | tf_op jit(solution)/shard_map/pallas_call | solution.py:204
  25.8 0.0 collective-permute-done.2.r3
  25.8 2.0 %collective-permute-done.3.r4 = bf16[128,1024]{1,0:T(8,128)(2,1)S(1)} collective-permute-done((bf16[128,1024]{1,0:T(8,128)(2,1)S(1)}, bf16[128,1024]{1,0:T(8,128)(2,1)S(1)}, u32[]{:S(2)}, u32[]{:S(2)}) %collective-permute-start.3) | collective-permute-done | bytes 262176 | tf_op jit(solution)/shard_map/ppermute | solution.py:232
  27.8 2.2 %shard_map.49 = bf16[256,2048]{1,0:T(8,128)(2,1)} custom-call(bf16[256,2048]{1,0:T(8,128)(2,1)S(1)} %copy-done, f32[2,128,768]{2,1,0:T(8,128)S(1)} %get-tuple-element.25.bias_ref, bf16[128,1024]{1,0:T(8,128)(2,1)S(1)} %collective-permute-done.r1, bf16[128,1024]{1,0:T(8,128)(2,1)S(1)} %collective-permute-done.1.r2, ...), custom_call_target="tpu_custom_call" | custom-call | tf_op jit(solution)/shard_map/pallas_call | solution.py:204
  (3 shorter events, 0.1 us)
Async XLA Ops:
  0.0 4.6 %copy-start = (bf16[256,2048]{1,0:T(8,128)(2,1)S(1)}, bf16[256,2048]{1,0:T(8,128)(2,1)}, u32[]{:S(2)}) copy-start(bf16[256,2048]{1,0:T(8,128)(2,1)} %q_ref.7) | copy-start | bytes 3145732
  0.0 4.6 %copy-start.1 = (s32[65536]{0:T(1024)S(1)}, s32[65536]{0:T(1024)}, u32[]{:S(2)}) copy-start(s32[65536]{0:T(1024)} %param.7) | copy-start | bytes 786436
  1.3 12.8 %collective-permute-start = (bf16[128,1024]{1,0:T(8,128)(2,1)S(1)}, bf16[128,1024]{1,0:T(8,128)(2,1)S(1)}, u32[]{:S(2)}, u32[]{:S(2)}) collective-permute-start(bf16[128,1024]{1,0:T(8,128)(2,1)S(1)} %pad_maximum_fusion.x1), channel_id=1, source_target_pairs={{0,1},{1,0},{2,6},{3,7},{4,5},{5,4},{6,10},{7,11},{8,9},{9,8},{10,... | collective-permute-start | bytes 786440 | tf_op jit(solution)/shard_map/ppermute | solution.py:232
  4.0 17.9 %collective-permute-start.1 = (bf16[128,1024]{1,0:T(8,128)(2,1)S(1)}, bf16[128,1024]{1,0:T(8,128)(2,1)S(1)}, u32[]{:S(2)}, u32[]{:S(2)}) collective-permute-start(bf16[128,1024]{1,0:T(8,128)(2,1)S(1)} %pad_maximum_fusion.1.x2), channel_id=1, source_target_pairs={{2,7},{3,6},{6,11},{7,10},{10,15},{11,14},{14,19},{15,18},{18,23},... | collective-permute-start | bytes 786440 | tf_op jit(solution)/shard_map/ppermute | solution.py:232
  6.6 19.3 %collective-permute-start.2 = (bf16[128,1024]{1,0:T(8,128)(2,1)S(1)}, bf16[128,1024]{1,0:T(8,128)(2,1)S(1)}, u32[]{:S(2)}, u32[]{:S(2)}) collective-permute-start(bf16[128,1024]{1,0:T(8,128)(2,1)S(1)} %pad_maximum_fusion.1.x2), channel_id=1, source_target_pairs={{0,4},{1,5},{2,3},{3,2},{4,8},{5,9},{6,7},{7,6},{8,12},{9,13},{10,... | collective-permute-start | bytes 786440 | tf_op jit(solution)/shard_map/ppermute | solution.py:232
  10.0 17.8 %collective-permute-start.3 = (bf16[128,1024]{1,0:T(8,128)(2,1)S(1)}, bf16[128,1024]{1,0:T(8,128)(2,1)S(1)}, u32[]{:S(2)}, u32[]{:S(2)}) collective-permute-start(bf16[128,1024]{1,0:T(8,128)(2,1)S(1)} %pad_maximum_fusion.x1), channel_id=1, source_target_pairs={{0,5},{1,4},{4,9},{5,8},{8,13},{9,12},{12,17},{13,16},{16,21},{17,... | collective-permute-start | bytes 786440 | tf_op jit(solution)/shard_map/ppermute | solution.py:232

commit v4 on v3

--- a/solution.py
+++ b/solution.py
@@ -179,9 +179,11 @@
                 for r in range(group):
                     cols = slice((g * group + r) * HD, (g * group + r + 1) * HD)
                     rows_ref[qb * HALF : (qb + 1) * HALF, cols] = res[r * HALF : (r + 1) * HALF]
-            cols = pl.ds(g * group * HD, group * HD)
-            copies.append(pltpu.make_async_copy(rows_ref.at[:, cols], out_ref.at[:, cols], sems.at[g]))
-            copies[-1].start()
+                if g == KV - 1 or qb == 1:
+                    rows = slice(qb * HALF if g == KV - 1 else 0, (qb + 1) * HALF)
+                    part = (rows, slice(g * group * HD, (g + 1) * group * HD))
+                    copies.append(pltpu.make_async_copy(rows_ref.at[part], out_ref.at[part], sems.at[g + qb * (g == KV - 1)]))
+                    copies[-1].start()
         far = jnp.logical_not(jnp.max(highest) <= FAR) if unmoved else None
         for copy in copies:
             copy.wait()
@@ -218,7 +220,7 @@
         queries,
         *args,
         out_specs=pl.BlockSpec(memory_space=pl.ANY),
-        scratch=[pltpu.VMEM(queries.shape, queries.dtype), pltpu.SemaphoreType.DMA((KV,))],
+        scratch=[pltpu.VMEM(queries.shape, queries.dtype), pltpu.SemaphoreType.DMA((KV + 1,))],
     )
 
 

time: 30.3 us -> 30.3 us (level)
  no operation moved by 1% of the time
where the time goes in v4:
time: 30.3 us; the launch traced here: 30 us
  starting transfers between devices  10.9 us (36%)
  blocking collectives  8.11 us (27%)
  Pallas kernels  7.56 us (25%)
  waiting for transfers between devices  1.97 us (7%)
  local copies, waits for them, and re-layouts  1.24 us (4%)
    ppermute x4, starting transfers between devices, send(): return lax.ppermute(x, BOTH, pairs)  10.9 us
    all_gather x2, blocking collectives, core_pair(): lax.all_gather(x, 'ctx', axis=0, tiled=True, axis_index_groups=[[i, i + 1...  8.11 us
    pallas_call x4, Pallas kernels, call(): pl.pallas_call(kernel, out_shape=outs, in_specs=[VMEM] * len(args), out_s...  7.56 us
    ppermute x4, waiting for transfers between devices, send(): return lax.ppermute(x, BOTH, pairs)  1.97 us
    dynamic_slice x1, local copies, waits for them, and re-layouts, columns(): return lax.dynamic_slice_in_dim(x, which * width, width, axis=1)  1.23 us
  transfers between devices with their start and end apart: 4, of which 1 were waited for; matrix products, arithmetic and copies ran while one was open for 0% of the time, Pallas kernels for 18%

profile of v4, /device:TPU:24, one launch (start us, length us, event | category | flops | bytes accessed | tf_op | source)
XLA Modules:
  0.0 30.0 jit_solution(11019121827824142558)
XLA Ops:
  0.0 0.0 copy-start
  0.0 0.0 copy-start.1
  0.0 1.2 %constant_dynamic-slice_fusion = (bf16[128,512]{1,0:T(8,128)(2,1)S(1)}, bf16[128,512]{1,0:T(8,128)(2,1)S(1)}, bf16[128,512]{1,0:T(8,128)(2,1)S(1)}, bf16[128,512]{1,0:T(8,128)(2,1)S(1)}) fusion(bf16[128,1024]{1,0:T(8,128)(2,1)} %param.6, s32[]{:T(128)S(6)} %select_n.26, s32[]{:T(128)S(6)} %select_n.25, bf16[128,1024]{1,0:T(8,128)(2,1)} %param.5), kind=kLoop, calls=%fused_computation.4 | loop fusion | bytes 1048584 | tf_op jit(solution)/shard_map/dynamic_slice | solution.py:247
  1.3 2.7 %collective-permute-start = (bf16[128,1024]{1,0:T(8,128)(2,1)S(1)}, bf16[128,1024]{1,0:T(8,128)(2,1)S(1)}, u32[]{:S(2)}, u32[]{:S(2)}) collective-permute-start(bf16[128,1024]{1,0:T(8,128)(2,1)S(1)} %pad_maximum_fusion.x1), channel_id=1, source_target_pairs={{0,1},{1,0},{2,6},{3,7},{4,5},{5,4},{6,10},{7,11},{8,9},{9,8},{10,... | collective-permute-start | bytes 786440 | tf_op jit(solution)/shard_map/ppermute | solution.py:234
  4.0 0.7 %collective-permute-start.1 = (bf16[128,1024]{1,0:T(8,128)(2,1)S(1)}, bf16[128,1024]{1,0:T(8,128)(2,1)S(1)}, u32[]{:S(2)}, u32[]{:S(2)}) collective-permute-start(bf16[128,1024]{1,0:T(8,128)(2,1)S(1)} %pad_maximum_fusion.1.x2), channel_id=1, source_target_pairs={{2,7},{3,6},{6,11},{7,10},{10,15},{11,14},{14,19},{15,18},{18,23},... | collective-permute-start | bytes 786440 | tf_op jit(solution)/shard_map/ppermute | solution.py:234
  4.6 0.0 copy-done
  4.6 0.0 copy-done.1
  4.7 1.9 %shard_map.46 = (f32[2,128,768]{2,1,0:T(8,128)S(1)}, f32[8,512,128]{2,1,0:T(8,128)S(1)}, f32[8,512,128]{2,1,0:T(8,128)S(1)}, f32[8,512,128]{2,1,0:T(8,128)S(1)}) custom-call(s32[512,128]{1,0:T(8,128)S(1)} %bitcast.1, bf16[256,2048]{1,0:T(8,128)(2,1)S(1)} %copy-done, bf16[128,1024]{1,0:T(8,128)(2,1)S(1)} %pad_maximum_fusion.x1, ...), custom_call_target="tpu_custom_call" | custom-call | tf_op jit(solution)/shard_map/pallas_call | solution.py:206
  6.6 3.4 %collective-permute-start.2 = (bf16[128,1024]{1,0:T(8,128)(2,1)S(1)}, bf16[128,1024]{1,0:T(8,128)(2,1)S(1)}, u32[]{:S(2)}, u32[]{:S(2)}) collective-permute-start(bf16[128,1024]{1,0:T(8,128)(2,1)S(1)} %pad_maximum_fusion.1.x2), channel_id=1, source_target_pairs={{0,4},{1,5},{2,3},{3,2},{4,8},{5,9},{6,7},{7,6},{8,12},{9,13},{10,... | collective-permute-start | bytes 786440 | tf_op jit(solution)/shard_map/ppermute | solution.py:234
  10.0 4.1 %collective-permute-start.3 = (bf16[128,1024]{1,0:T(8,128)(2,1)S(1)}, bf16[128,1024]{1,0:T(8,128)(2,1)S(1)}, u32[]{:S(2)}, u32[]{:S(2)}) collective-permute-start(bf16[128,1024]{1,0:T(8,128)(2,1)S(1)} %pad_maximum_fusion.x1), channel_id=1, source_target_pairs={{0,5},{1,4},{4,9},{5,8},{8,13},{9,12},{12,17},{13,16},{16,21},{17,... | collective-permute-start | bytes 786440 | tf_op jit(solution)/shard_map/ppermute | solution.py:234
  14.1 0.0 collective-permute-done.r1
  14.1 1.8 %shard_map.47 = (f32[8,512,128]{2,1,0:T(8,128)S(1)}, f32[8,512,128]{2,1,0:T(8,128)S(1)}, f32[8,512,128]{2,1,0:T(8,128)S(1)}) custom-call(bf16[256,2048]{1,0:T(8,128)(2,1)S(1)} %copy-done, f32[2,128,768]{2,1,0:T(8,128)S(1)} %get-tuple-element.25.bias_ref, bf16[128,1024]{1,0:T(8,128)(2,1)S(1)} %pad_maximum_fusion.1.x2, ...), custom_call_target="tpu_custom_call" | custom-call | tf_op jit(solution)/shard_map/pallas_call | solution.py:206
  15.9 0.1 broadcast_select_fusion.1
  15.9 5.9 %all_gather.6.near_pair = bf16[256,1024]{1,0:T(8,128)(2,1)S(1)} all-gather(bf16[128,1024]{1,0:T(8,128)(2,1)S(1)} %broadcast_select_fusion.1), channel_id=1, replica_groups={{0,2},{4,6},{8,10},{12,14},{16,18},{20,22},{24,26},{28,30},{32,34},{36,..., dimensions={0}, use_global_device_ids=true | all-gather | bytes 786432 | tf_op jit(solution)/shard_map/all_gather | solution.py:239
  21.9 0.0 collective-permute-done.1.r2
  21.9 2.2 %all_gather.7.cross_pair = bf16[256,1024]{1,0:T(8,128)(2,1)S(1)} all-gather(bf16[128,1024]{1,0:T(8,128)(2,1)S(1)} %broadcast_select_fusion), channel_id=1, replica_groups={{0,2},{4,6},{8,10},{12,14},{16,18},{20,22},{24,26},{28,30},{32,34},{36,..., dimensions={0}, use_global_device_ids=true | all-gather | bytes 786432 | tf_op jit(solution)/shard_map/all_gather | solution.py:239
  24.1 1.7 %shard_map.48 = (f32[8,512,128]{2,1,0:T(8,128)S(1)}, f32[8,512,128]{2,1,0:T(8,128)S(1)}, f32[8,512,128]{2,1,0:T(8,128)S(1)}) custom-call(bf16[256,2048]{1,0:T(8,128)(2,1)S(1)} %copy-done, f32[2,128,768]{2,1,0:T(8,128)S(1)} %get-tuple-element.25.bias_ref, bf16[256,1024]{1,0:T(8,128)(2,1)S(1)} %all_gather.6.near_pair, ...), custom_call_target="tpu_custom_call" | custom-call | tf_op jit(solution)/shard_map/pallas_call | solution.py:206
  25.8 0.0 collective-permute-done.2.r3
  25.8 2.0 %collective-permute-done.3.r4 = bf16[128,1024]{1,0:T(8,128)(2,1)S(1)} collective-permute-done((bf16[128,1024]{1,0:T(8,128)(2,1)S(1)}, bf16[128,1024]{1,0:T(8,128)(2,1)S(1)}, u32[]{:S(2)}, u32[]{:S(2)}) %collective-permute-start.3) | collective-permute-done | bytes 262176 | tf_op jit(solution)/shard_map/ppermute | solution.py:234
  27.8 2.2 %shard_map.49 = bf16[256,2048]{1,0:T(8,128)(2,1)} custom-call(bf16[256,2048]{1,0:T(8,128)(2,1)S(1)} %copy-done, f32[2,128,768]{2,1,0:T(8,128)S(1)} %get-tuple-element.25.bias_ref, bf16[128,1024]{1,0:T(8,128)(2,1)S(1)} %collective-permute-done.r1, bf16[128,1024]{1,0:T(8,128)(2,1)S(1)} %collective-permute-done.1.r2, ...), custom_call_target="tpu_custom_call" | custom-call | tf_op jit(solution)/shard_map/pallas_call | solution.py:206
  (3 shorter events, 0.1 us)
Async XLA Ops:
  0.0 4.6 %copy-start = (bf16[256,2048]{1,0:T(8,128)(2,1)S(1)}, bf16[256,2048]{1,0:T(8,128)(2,1)}, u32[]{:S(2)}) copy-start(bf16[256,2048]{1,0:T(8,128)(2,1)} %q_ref.7) | copy-start | bytes 3145732
  0.0 4.6 %copy-start.1 = (s32[65536]{0:T(1024)S(1)}, s32[65536]{0:T(1024)}, u32[]{:S(2)}) copy-start(s32[65536]{0:T(1024)} %param.7) | copy-start | bytes 786436
  1.3 12.8 %collective-permute-start = (bf16[128,1024]{1,0:T(8,128)(2,1)S(1)}, bf16[128,1024]{1,0:T(8,128)(2,1)S(1)}, u32[]{:S(2)}, u32[]{:S(2)}) collective-permute-start(bf16[128,1024]{1,0:T(8,128)(2,1)S(1)} %pad_maximum_fusion.x1), channel_id=1, source_target_pairs={{0,1},{1,0},{2,6},{3,7},{4,5},{5,4},{6,10},{7,11},{8,9},{9,8},{10,... | collective-permute-start | bytes 786440 | tf_op jit(solution)/shard_map/ppermute | solution.py:234
  4.0 17.9 %collective-permute-start.1 = (bf16[128,1024]{1,0:T(8,128)(2,1)S(1)}, bf16[128,1024]{1,0:T(8,128)(2,1)S(1)}, u32[]{:S(2)}, u32[]{:S(2)}) collective-permute-start(bf16[128,1024]{1,0:T(8,128)(2,1)S(1)} %pad_maximum_fusion.1.x2), channel_id=1, source_target_pairs={{2,7},{3,6},{6,11},{7,10},{10,15},{11,14},{14,19},{15,18},{18,23},... | collective-permute-start | bytes 786440 | tf_op jit(solution)/shard_map/ppermute | solution.py:234
  6.6 19.3 %collective-permute-start.2 = (bf16[128,1024]{1,0:T(8,128)(2,1)S(1)}, bf16[128,1024]{1,0:T(8,128)(2,1)S(1)}, u32[]{:S(2)}, u32[]{:S(2)}) collective-permute-start(bf16[128,1024]{1,0:T(8,128)(2,1)S(1)} %pad_maximum_fusion.1.x2), channel_id=1, source_target_pairs={{0,4},{1,5},{2,3},{3,2},{4,8},{5,9},{6,7},{7,6},{8,12},{9,13},{10,... | collective-permute-start | bytes 786440 | tf_op jit(solution)/shard_map/ppermute | solution.py:234
  10.0 17.8 %collective-permute-start.3 = (bf16[128,1024]{1,0:T(8,128)(2,1)S(1)}, bf16[128,1024]{1,0:T(8,128)(2,1)S(1)}, u32[]{:S(2)}, u32[]{:S(2)}) collective-permute-start(bf16[128,1024]{1,0:T(8,128)(2,1)S(1)} %pad_maximum_fusion.x1), channel_id=1, source_target_pairs={{0,5},{1,4},{4,9},{5,8},{8,13},{9,12},{12,17},{13,16},{16,21},{17,... | collective-permute-start | bytes 786440 | tf_op jit(solution)/shard_map/ppermute | solution.py:234
